TPU v7x, 256 devices: a whole 4x4x8 slice. The times are simulated.
256 devices in a mesh: tm: 32 (over z, y), feat: 8 (over x, core).
Axes of the slice: x: 4, y: 4, z: 8, core: 2. Of those that a mesh axis runs over, the one named last changes fastest.
Arguments:
- tile_data: bfloat16 [2048, 32, 128, 128], P('tm', 'feat'), may hold values from -1 to 1
- tile_ids: int32 [2048, 32], P('tm', 'feat'), may hold values from 0 to 31, as said below
- owner_perm: int32 [2048], P('tm'), may hold values from 0 to 2047, as said below
- events: int32 [2048, 128], P('tm'), may hold values 0 or 1
- groups: int32 [2048, 128], P('tm'), may hold values from 0 to 127, as said below
- coefficients: bfloat16 [32768], P('feat'), may hold values from -4 to 4
Outputs:
- gradient: float32 [32768], P('feat')
- newton_step: float32 [32768], P('feat')
Inputs may be any that keep to these rules, and one draw needn't show every extreme that they name: `tile_ids`: in each feature shard's 4 columns a row block names 4 different local feature blocks. `owner_perm`: A permutation of row blocks; each patient shard of 64 row blocks sends exactly 2 of them to each time shard. `groups`: group numbers start at 0 in every row block and never fall within it; a tied group never spans two row blocks.
All inputs are finite; a program needn't handle non-finite values. No bound on the sum of `events` on one device may be relied on, other than what follows from the above.
Results may differ from a plain program's by a relative error of at most 0.00035.
The roundings to bfloat16 on the way count: a program that leaves them out, or rounds other values in their place, can miss the bound.
Values may be sent and summed in bfloat16 or wider, within the bound.
A program may use at most 128 MiB of HBM per device.

v0:
```python
import jax
import jax.numpy as jnp
from jax import lax
from jax.sharding import PartitionSpec as P

ridge_weight = 1.0


def entering(part, axis, combine, identity, reverse):
    count = lax.axis_size(axis)
    place = lax.axis_index(axis)
    ahead = count - 1 - place if reverse else place
    gathered = jax.tree.map(lambda a: lax.all_gather(a, axis), part)
    state = jax.tree.map(lambda a, e: jnp.zeros_like(a) + jnp.asarray(e, a.dtype), part, identity)

    def one(turn, state):
        source = count - 1 - turn if reverse else turn
        return combine(
            state, jax.tree.map(lambda a: lax.dynamic_index_in_dim(a, source, 0, False), gathered)
        )

    return lax.fori_loop(0, ahead, one, state)


def add_pair(earlier, later):
    return (earlier[0] + later[0], earlier[1] + later[1])


def add_one(earlier, later):
    return earlier + later


def solve_blocks(grad_blocks, hess_blocks):
    tile_width = hess_blocks.shape[1]
    system = hess_blocks + ridge_weight * jnp.eye(tile_width, dtype=jnp.float32)[None]
    factor = jnp.linalg.cholesky(system)
    return jax.scipy.linalg.cho_solve((factor, True), grad_blocks[:, :, None])[:, :, 0]


def local(tile_data, tile_ids, owner_perm, events, groups, coefficients):
    row_count = tile_data.shape[0]
    tile_width = tile_data.shape[2]
    shard_count = lax.axis_size("tm")
    per_pair = row_count // shard_count
    local_blocks = coefficients.shape[0] // tile_width
    coef_blocks = coefficients.reshape(local_blocks, tile_width)
    block_range = jnp.arange(local_blocks, dtype=jnp.int32)
    target = owner_perm // row_count
    arrival_slot = owner_perm % row_count
    sorting = jnp.argsort(target, stable=True)
    outgoing = (
        tile_data[sorting].reshape(
            shard_count, per_pair, tile_data.shape[1], tile_width, tile_width
        ),
        tile_ids[sorting].reshape(shard_count, per_pair, tile_ids.shape[1]),
        events[sorting].reshape(shard_count, per_pair, tile_width),
        arrival_slot[sorting].reshape(shard_count, per_pair),
    )
    received = (
        lax.all_to_all(outgoing[0], "tm", split_axis=0, concat_axis=0, tiled=True),
        lax.all_to_all(outgoing[1], "tm", split_axis=0, concat_axis=0, tiled=True),
        lax.all_to_all(outgoing[2], "tm", split_axis=0, concat_axis=0, tiled=True),
        lax.all_to_all(outgoing[3], "tm", split_axis=0, concat_axis=0, tiled=True),
    )
    arrival = received[3].reshape(row_count)
    restore_order = jnp.argsort(arrival)
    time_tiles = received[0].reshape(row_count, tile_data.shape[1], tile_width, tile_width)[
        restore_order
    ]
    time_ids = received[1].reshape(row_count, tile_ids.shape[1])[restore_order]
    time_events = received[2].reshape(row_count, tile_width)[restore_order]
    onehot = (time_ids[:, :, None] == block_range[None, None, :]).astype(jnp.bfloat16)
    picked = jnp.einsum(
        "nsj,jt->nst", onehot, coef_blocks, preferred_element_type=jnp.float32
    ).astype(jnp.bfloat16)
    time_eta = lax.psum(
        jnp.einsum("nspt,nst->np", time_tiles, picked, preferred_element_type=jnp.float32), "feat"
    )
    event_flag = time_events.astype(jnp.float32)
    risk_score = jnp.exp(time_eta)
    later_mask = (groups[:, None, :] >= groups[:, :, None]).astype(jnp.float32)
    later_in = jnp.einsum("bik,bk->bi", later_mask, risk_score, precision=lax.Precision.HIGHEST)
    block_tot = jnp.sum(risk_score, axis=1)
    device_tot = jnp.sum(block_tot)
    after_device = entering(device_tot, "tm", add_one, jnp.zeros((), jnp.float32), True)
    after_blocks = jnp.concatenate(
        [jnp.cumsum(block_tot[::-1])[::-1][1:], jnp.zeros((1,), jnp.float32)]
    )
    risk_total = after_device + after_blocks[:, None] + later_in
    hazard_one = event_flag / risk_total
    hazard_two = hazard_one / risk_total
    earlier_one = jnp.einsum("bki,bk->bi", later_mask, hazard_one, precision=lax.Precision.HIGHEST)
    earlier_two = jnp.einsum("bki,bk->bi", later_mask, hazard_two, precision=lax.Precision.HIGHEST)
    tot_one = jnp.sum(hazard_one, axis=1)
    tot_two = jnp.sum(hazard_two, axis=1)
    zero_scalar = jnp.zeros((), jnp.float32)
    before_dev = entering(
        (jnp.sum(tot_one), jnp.sum(tot_two)), "tm", add_pair, (zero_scalar, zero_scalar), False
    )
    before_one = jnp.concatenate([jnp.zeros((1,), jnp.float32), jnp.cumsum(tot_one)[:-1]])
    before_two = jnp.concatenate([jnp.zeros((1,), jnp.float32), jnp.cumsum(tot_two)[:-1]])
    cum_one = before_dev[0] + before_one[:, None] + earlier_one
    cum_two = before_dev[1] + before_two[:, None] + earlier_two
    residual = event_flag - risk_score * cum_one
    weight = risk_score * cum_one - risk_score * risk_score * cum_two
    residual, weight = (residual, weight)
    resid_round = residual.astype(jnp.bfloat16)
    weighted = (time_tiles * weight[:, None, :, None]).astype(jnp.bfloat16)
    grad_slots = jnp.einsum(
        "nspa,np->nsa", time_tiles, resid_round, preferred_element_type=jnp.float32
    )
    hess_slots = jnp.einsum(
        "nspa,nspb->nsab", weighted, time_tiles, preferred_element_type=jnp.float32
    )
    flat_ids = time_ids.reshape(-1)
    grad_local = (
        jnp.zeros((local_blocks, tile_width), jnp.float32)
        .at[flat_ids]
        .add(grad_slots.reshape(-1, tile_width))
    )
    hess_local = (
        jnp.zeros((local_blocks, tile_width, tile_width), jnp.float32)
        .at[flat_ids]
        .add(hess_slots.reshape(-1, tile_width, tile_width))
    )
    grad_local, hess_local = (grad_local, hess_local)
    grad_part, hess_part = (
        lax.psum_scatter(grad_local, "tm", scatter_dimension=0, tiled=True),
        lax.psum_scatter(hess_local, "tm", scatter_dimension=0, tiled=True),
    )
    step_part = solve_blocks(grad_part, hess_part)
    gradient, newton_step = (
        lax.all_gather(grad_part, "tm", axis=0, tiled=True),
        lax.all_gather(step_part, "tm", axis=0, tiled=True),
    )
    return (gradient.reshape(-1), newton_step.reshape(-1))


def solution(mesh):
    return jax.shard_map(
        local,
        mesh=mesh,
        in_specs=(
            P("tm", "feat", None, None),
            P("tm", "feat"),
            P("tm"),
            P("tm", None),
            P("tm", None),
            P("feat"),
        ),
        out_specs=(P("feat"), P("feat")),
        check_vma=False,
    )
```

profile of v0, /device:TPU:8, one launch (start us, length us, event | category | flops | bytes accessed | tf_op | source)
XLA Modules:
  0.0 893.0 jit_solution(6770830898521049463)
XLA Ops:
  11.4 11.7 %all-to-all-start.1 = ((s32[32,1,2]{2,1,0:T(1,128)}), s32[32,1,2]{2,1,0:T(1,128)S(1)}, u32[]{:S(2)}, u32[]{:S(2)}) async-start(s32[32,1,2]{2,1,0:T(1,128)} %bitcast.5), calls=%async_computation.1 | async-start | bytes 32768 | tf_op jit(solution)/shard_map/all_to_all | solution.py:63
  25.1 6.5 all-to-all-done.1
  31.6 4.9 all-to-all-start
  37.7 7.5 all-to-all-done
  45.2 4.9 all-to-all-start.3
  50.1 8.9 gather_fusion.3
  59.0 10.1 %all-to-all-start.2 = ((bf16[32,2,4,128,128]{4,3,2,1,0:T(8,128)(2,1)}), bf16[32,2,4,128,128]{4,3,2,1,0:T(8,128)(2,1)}, u32[]{:S(2)}, u32[]{:S(2)}) async-start(bf16[32,2,4,128,128]{4,3,2,1,0:T(8,128)(2,1)} %bitcast.89), calls=%async_computation.2 | async-start | bytes 16777216 | tf_op jit(solution)/shard_map/all_to_all | solution.py:60
  74.9 176.5 %all-to-all-done.2 = bf16[32,2,4,128,128]{4,3,2,1,0:T(8,128)(2,1)} async-done(((bf16[32,2,4,128,128]{4,3,2,1,0:T(8,128)(2,1)}), bf16[32,2,4,128,128]{4,3,2,1,0:T(8,128)(2,1)}, u32[]{:S(2)}, u32[]{:S(2)}) %all-to-all-start.2) | async-done | bytes 8388640 | tf_op jit(solution)/shard_map/all_to_all | solution.py:60
  251.4 8.9 gather_fusion.4
  260.3 5.6 fusion.15
  265.9 24.8 %psum.7 = f32[64,128]{1,0:T(8,128)S(1)} all-reduce(f32[64,128]{1,0:T(8,128)S(1)} %bitcast.96), channel_id=1, replica_groups=mesh['tm'=32,'feat'=8] {'feat'}, use_global_device_ids=true, to_apply=%region_2.3 | all-reduce | flops 8192 | bytes 65536 | tf_op jit(solution)/shard_map/psum | solution.py:76
  292.7 66.3 %all-reduce = f32[32]{0:T(128)S(1)} all-reduce(f32[32]{0:T(128)S(1)} %dynamic-update-slice.3), channel_id=1, replica_groups=mesh['tm'=32,'feat'=8] {'tm'}, use_global_device_ids=true, to_apply=%add | all-reduce | flops 32 | bytes 256
  359.1 37.8 %while.24 = (s32[]{:T(128)}, f32[]{:T(128)}, s32[]{:T(128)}, f32[32]{0:T(128)S(1)}, s32[]{:T(128)}, /*index=5*/s32[]{:T(128)}, s32[]{:T(128)}, s32[]{:T(128)}) while((s32[]{:T(128)}, f32[]{:T(128)}, s32[]{:T(128)}, f32[32]{0:T(128)S(1)}, s32[]{:T(128)}, /*index=5*/s32[]{:T(128)}, s32[]{:T(128)}, s32[]{:T(128)}) %tuple.56), condition=%wide.region_5.6_spmd, body=%wide.region_4.5_spmd.sunk | while | flops 7 | bytes 163 | solution.py:22
  397.3 4.0 fusion.6
  410.6 76.2 %all-reduce.4 = (f32[32]{0:T(128)S(1)}, f32[32]{0:T(128)S(1)}) all-reduce(f32[32]{0:T(128)S(1)} %dynamic-update-slice.4, f32[32]{0:T(128)S(1)} %dynamic-update-slice.5), channel_id=1, replica_groups=mesh['tm'=32,'feat'=8] {'tm'}, use_global_device_ids=true, to_apply=%add.1 | all-reduce | flops 64 | bytes 512
  490.3 13.4 %fusion = f32[64,4,128,128]{3,2,1,0:T(8,128)} fusion(bf16[64,4,128,128]{3,2,1,0:T(8,128)(2,1)} %gather_fusion.4, f32[64,128]{1,0:T(8,128)S(1)} %get-tuple-element.129), kind=kOutput, calls=%fused_computation.10 | convolution fusion | flops 1086324736 | bytes 25198592 | tf_op jit(solution)/shard_map/nspa,nspb->nsab/dot_general | solution.py:112
  504.0 33.2 %scatter_fusion = f32[32,128,128]{2,1,0:T(8,128)S(1)} fusion(f32[32,128,128]{2,1,0:T(8,128)S(1)} %broadcast_in_dim.14, s32[256]{0:T(256)S(1)} %bitcast.102, f32[256,128,128]{2,1,0:T(8,128)} %bitcast.88), kind=kCustom, calls=%fused_computation.8 | custom fusion | flops 4194304 | bytes 50332672 | tf_op jit(solution)/shard_map/scatter-add | solution.py:124
  538.6 4.6 fusion.20
  544.6 209.6 %all-reduce.3 = f32[32,128]{1,0:T(8,128)S(1)} all-reduce(f32[32,128]{1,0:T(8,128)S(1)} %scatter_custom_fusion), channel_id=3, replica_groups=mesh['tm'=32,'feat'=8] {'tm'}, use_global_device_ids=true, to_apply=%region_15.16.clone | all-reduce | flops 4096 | bytes 32768
  754.9 40.1 %all-gather.1 = f32[32,1,128]{2,1,0:T(1,128)S(1)} all-gather(f32[1,1,128]{2,1,0:T(1,128)S(1)} %fusion.30), channel_id=1, replica_groups=mesh['tm'=32,'feat'=8] {'tm'}, dimensions={0}, use_global_device_ids=true | all-gather | bytes 16896 | tf_op jit(solution)/shard_map/all_gather | solution.py:133
  795.0 26.4 %reduce-scatter.2.cloned.1.call-done = f32[1,128,128]{2,1,0:T(8,128)} async-done(((f32[32,128,128]{2,1,0:T(8,128)}), f32[1,128,128]{2,1,0:T(8,128)}) %reduce-scatter.2.cloned.1.call-update) | async-done | bytes 65552 | tf_op jit(solution)/shard_map/reduce_scatter | solution.py:129
  823.2 11.7 %custom-call.11 = f32[1,128,128]{2,1,0:T(8,128)S(1)} custom-call(f32[1,128,128]{2,1,0:T(8,128)S(1)} %fusion.19), custom_call_target="Cholesky" | custom-call | tf_op jit(solution)/shard_map/jit(cholesky)/cholesky | solution.py:36
  836.2 9.8 %custom-call.12 = f32[1,128,128]{1,2,0:T(8,128)S(1)} custom-call(f32[1,128,128]{2,1,0:T(8,128)S(1)} %select_select_fusion), custom_call_target="InvertDiagBlocksLowerTriangular" | custom-call | tf_op jit(solution)/shard_map/jit(_cho_solve)/triangular_solve | solution.py:37
  847.1 37.9 %all-gather.2 = f32[32,1,128]{2,1,0:T(1,128)S(1)} all-gather(f32[1,1,128]{2,1,0:T(1,128)S(1)} %convolution_bitcast_fusion), channel_id=2, replica_groups=mesh['tm'=32,'feat'=8] {'tm'}, dimensions={0}, use_global_device_ids=true | all-gather | bytes 16896 | tf_op jit(solution)/shard_map/all_gather | solution.py:134
  (107 shorter events, 56.2 us)
Async XLA Ops:
  7.2 29.3 %copy-start = (s32[64,128]{1,0:T(8,128)S(1)}, s32[64,128]{1,0:T(8,128)}, u32[]{:S(2)}) copy-start(s32[64,128]{1,0:T(8,128)} %param.13) | copy-start | bytes 98308
  11.4 20.2 %all-to-all-start.1 = ((s32[32,1,2]{2,1,0:T(1,128)}), s32[32,1,2]{2,1,0:T(1,128)S(1)}, u32[]{:S(2)}, u32[]{:S(2)}) async-start(s32[32,1,2]{2,1,0:T(1,128)} %bitcast.5), calls=%async_computation.1 | async-start | bytes 32768 | tf_op jit(solution)/shard_map/all_to_all | solution.py:63
  31.6 13.7 %all-to-all-start = ((s32[32,2,4]{2,1,0:T(2,128)}), s32[32,2,4]{2,1,0:T(2,128)S(1)}, u32[]{:S(2)}, u32[]{:S(2)}) async-start(s32[32,2,4]{2,1,0:T(2,128)} %bitcast.3), calls=%async_computation | async-start | bytes 65536 | tf_op jit(solution)/shard_map/all_to_all | solution.py:61
  45.2 13.8 %all-to-all-start.3 = ((s32[32,2,128]{2,1,0:T(2,128)}), s32[32,2,128]{2,1,0:T(2,128)S(1)}, u32[]{:S(2)}, u32[]{:S(2)}) async-start(s32[32,2,128]{2,1,0:T(2,128)} %bitcast.9), calls=%async_computation.3 | async-start | bytes 65536 | tf_op jit(solution)/shard_map/all_to_all | solution.py:62
  59.0 10.2 %copy-start.3 = (u32[256]{0:T(256)S(1)}, u32[256]{0:T(256)}, u32[]{:S(2)}) copy-start(u32[256]{0:T(256)} %constant.148) | copy-start | bytes 3076
  59.0 15.0 %copy-start.2 = (bf16[4096]{0:T(1024)(128)(2,1)S(1)}, bf16[4096]{0:T(1024)(128)(2,1)}, u32[]{:S(2)}) copy-start(bf16[4096]{0:T(1024)(128)(2,1)} %param.15) | copy-start | bytes 24580
  59.0 192.3 %all-to-all-start.2 = ((bf16[32,2,4,128,128]{4,3,2,1,0:T(8,128)(2,1)}), bf16[32,2,4,128,128]{4,3,2,1,0:T(8,128)(2,1)}, u32[]{:S(2)}, u32[]{:S(2)}) async-start(bf16[32,2,4,128,128]{4,3,2,1,0:T(8,128)(2,1)} %bitcast.89), calls=%async_computation.2 | async-start | bytes 16777216 | tf_op jit(solution)/shard_map/all_to_all | solution.py:60
  69.1 752.2 %reduce-scatter.2.cloned.1.call-start = ((), (), s32[]{:S(2)}) async-start(), calls=%async_computation.5 | async-start | bytes 2162688 | tf_op jit(solution)/shard_map/reduce_scatter | solution.py:129
  260.3 137.0 %copy-start.4 = (s32[64,128]{1,0:T(8,128)S(1)}, s32[64,128]{1,0:T(8,128)}, u32[]{:S(2)}) copy-start(s32[64,128]{1,0:T(8,128)} %param.14) | copy-start | bytes 98308
  537.2 1.4 copy-start.1
Sparse Core Ops, SparseCore 0:
  538.7 282.6 reduce-scatter.1
where the time goes:
time: 896 us; the launch traced here: 893 us
  blocking collectives  455 us (51%)
  waiting for transfers between devices  217 us (24%)
  other arithmetic  66.5 us (7%)
  local copies, waits for them, and re-layouts  52.4 us (6%)
  matrix products  34.7 us (4%)
  starting transfers between devices  31.6 us (4%)
  loops' own time  21.7 us (2%)
  between operations  14.3 us (2%)
    unnamed x3, blocking collectives  352 us
    all_to_all x1, waiting for transfers between devices, local(): lax.all_to_all(outgoing[0], 'tm', split_axis=0, concat_axis=0, tiled=True)  177 us
    all_gather x1, blocking collectives, local(): lax.all_gather(grad_part, 'tm', axis=0, tiled=True)  40.1 us
    all_gather x1, blocking collectives, local(): lax.all_gather(step_part, 'tm', axis=0, tiled=True)  37.9 us
    scatter-add x1, other arithmetic, local(): hess_local = jnp.zeros((local_blocks, tile_width, tile_width), jnp.float3...  33.2 us
    reduce_scatter x1, waiting for transfers between devices, local(): lax.psum_scatter(hess_local, 'tm', scatter_dimension=0, tiled=True)  26.4 us
    psum x1, blocking collectives, local(): lax.psum(jnp.einsum('nspt,nst->np', time_tiles, picked, preferred_element...  24.8 us
    another operation x2, loops' own time, entering(): return lax.fori_loop(0, ahead, one, state)  21.7 us
  transfers between devices with their start and end apart: 5, of which 4 were waited for; matrix products, arithmetic and copies ran while one was open for 3% of the time, Pallas kernels for 0%

commit v1 on v0

v1 whole, which is shorter than its diff:
```python
import functools
import math

import jax
import jax.numpy as jnp
from jax import lax
from jax.experimental import pallas as pl
from jax.experimental.pallas import tpu as pltpu
from jax.sharding import PartitionSpec as P

MESH = pl.DeviceIdType.MESH
TILE = 128
HALF = 64
PACK = 72
SHIFTS = (1, 2, 4, 8, 16, 32, 64)
Y_SIZE = 4
CHUNKS = 4


def lanes_of(rows):
    return lax.broadcasted_iota(jnp.int32, (rows, TILE), 1)


def scores_kernel(
    n_tm, n_feat,
    tiles, ids, perm_row, events, groups, coef,
    resid_out, weight_out,
    held, eta_parts, perm_all, group_send, group_recv, sum_one, sum_two, pay_one, pay_two, shifted,
    tile_sem, eta_send, eta_recv, perm_send, perm_recv, grp_send, grp_recv,
    one_send, one_recv, two_send, two_recv,
):
    me = lax.axis_index("tm")
    mf = lax.axis_index("feat")
    rows = events.shape[0]
    per = rows // CHUNKS
    slots = tiles.shape[1]

    def tile_copy(q):
        part = pl.ds(q * per, per)
        return pltpu.make_async_copy(tiles.at[part], held.at[part], tile_sem.at[q])

    for q in range(CHUNKS):
        tile_copy(q).start()

    barrier = pltpu.get_barrier_semaphore()

    def greet_tm(i, c):
        pl.semaphore_signal(
            barrier, inc=1, device_id=(lax.rem(me + i, n_tm), mf), device_id_type=MESH
        )
        return c

    def greet_feat(i, c):
        pl.semaphore_signal(
            barrier, inc=1, device_id=(me, lax.rem(mf + i, n_feat)), device_id_type=MESH
        )
        return c

    lax.fori_loop(1, n_tm, greet_tm, 0)
    lax.fori_loop(1, n_feat, greet_feat, 0)
    pl.semaphore_wait(barrier, n_tm + n_feat - 2)

    def tm_send(src_of, dst, send_sem, recv_sem):
        def one(i, c):
            peer = lax.rem(me + i, n_tm)
            pltpu.make_async_remote_copy(
                src_ref=src_of(peer), dst_ref=dst.at[me],
                send_sem=send_sem.at[peer], recv_sem=recv_sem.at[me],
                device_id=(peer, mf), device_id_type=MESH,
            ).start()
            return c

        lax.fori_loop(1, n_tm, one, 0)

    def tm_wait(src_of, dst, send_sem, recv_sem):
        def one(i, c):
            peer = lax.rem(me + i, n_tm)
            copy = pltpu.make_async_remote_copy(
                src_ref=src_of(peer), dst_ref=dst.at[peer],
                send_sem=send_sem.at[peer], recv_sem=recv_sem.at[peer],
                device_id=(peer, mf), device_id_type=MESH,
            )
            copy.wait_recv()
            copy.wait_send()
            return c

        lax.fori_loop(1, n_tm, one, 0)

    perm_all[me] = perm_row[...]
    tm_send(lambda peer: perm_row, perm_all, perm_send, perm_recv)

    chunk_lane = lanes_of(TILE)

    def eta_copy(q, peer, slot):
        part = pl.ds(q * per, per)
        return pltpu.make_async_remote_copy(
            src_ref=eta_parts.at[mf, part], dst_ref=eta_parts.at[slot, part],
            send_sem=eta_send.at[q, peer], recv_sem=eta_recv.at[q, slot],
            device_id=(me, peer), device_id_type=MESH,
        )

    def eta_chunk(q):
        tile_copy(q).wait()

        def one(i, kept):
            n = q * per + i
            total = held[n, 0].astype(jnp.float32) * coef[ids[n, 0]]
            for s in range(1, slots):
                total = total + held[n, s].astype(jnp.float32) * coef[ids[n, s]]
            column = jnp.sum(total, axis=1, keepdims=True)
            return jnp.where(chunk_lane == i, column, kept)

        columns = lax.fori_loop(0, per, one, jnp.zeros((TILE, TILE), jnp.float32))
        eta_parts[mf, q * per : (q + 1) * per, :] = columns.T[:per, :]

        def send(i, c):
            eta_copy(q, lax.rem(mf + i, n_feat), mf).start()
            return c

        lax.fori_loop(1, n_feat, send, 0)

    lane = lanes_of(rows)
    row = lax.broadcasted_iota(jnp.int32, (rows, TILE), 0)
    diagonal = lane == row
    perm_col = jnp.sum(
        jnp.where(diagonal, perm_row[...], 0.0), axis=1, keepdims=True
    )

    eta_chunk(0)

    tm_wait(lambda peer: perm_row, perm_all, perm_send, perm_recv)
    every = perm_all[:, 0, :]
    shard = jnp.floor(every * (1.0 / rows))
    within = every - shard * rows
    mine = jnp.logical_and(shard == me.astype(jnp.float32), lanes_of(n_tm) < rows)
    low = jnp.min(jnp.where(mine, within, 4096.0), axis=1, keepdims=True)
    high = jnp.max(jnp.where(mine, within, -1.0), axis=1, keepdims=True)
    place = lax.broadcasted_iota(jnp.int32, (n_tm, rows), 1).astype(jnp.float32)
    group_bf = groups[...].astype(jnp.float32).astype(jnp.bfloat16)
    first = jnp.dot(
        jnp.where(place == low, 1.0, 0.0).astype(jnp.bfloat16), group_bf,
        preferred_element_type=jnp.float32,
    )
    second = jnp.dot(
        jnp.where(place == high, 1.0, 0.0).astype(jnp.bfloat16), group_bf,
        preferred_element_type=jnp.float32,
    )
    for c in range(n_tm):
        group_send[c, :, 0:TILE] = first[c : c + 1, :]
        group_send[c, :, TILE : 2 * TILE] = second[c : c + 1, :]
    group_recv[me] = group_send[me]
    tm_send(lambda peer: group_send.at[peer], group_recv, grp_send, grp_recv)

    for q in range(1, CHUNKS):
        eta_chunk(q)

    tm_wait(lambda peer: group_send.at[peer], group_recv, grp_send, grp_recv)
    my_shard = jnp.floor(perm_col * (1.0 / rows))
    same = jnp.logical_and(
        jnp.floor(perm_row[...] * (1.0 / rows)) == my_shard, perm_row[...] < perm_col
    )
    rank = jnp.sum(
        jnp.where(jnp.logical_and(same, lane < rows), 1.0, 0.0), axis=1, keepdims=True
    )
    shard_lane = lax.broadcasted_iota(jnp.int32, (rows, n_tm), 1).astype(jnp.float32)
    hit = jnp.where(shard_lane == my_shard, 1.0, 0.0)
    cohort_groups = jnp.dot(
        (hit * (1.0 - rank)).astype(jnp.bfloat16),
        group_recv[:, 0, 0:TILE].astype(jnp.bfloat16),
        preferred_element_type=jnp.float32,
    ) + jnp.dot(
        (hit * rank).astype(jnp.bfloat16),
        group_recv[:, 0, TILE : 2 * TILE].astype(jnp.bfloat16),
        preferred_element_type=jnp.float32,
    )
    for k, d in enumerate(SHIFTS):
        back = pltpu.roll(cohort_groups, d, 1)
        shifted[k] = jnp.where(jnp.logical_and(lane >= d, back == cohort_groups), 1.0, 0.0)
        ahead = pltpu.roll(cohort_groups, TILE - d, 1)
        shifted[len(SHIFTS) + k] = jnp.where(
            jnp.logical_and(lane < TILE - d, ahead == cohort_groups), 1.0, 0.0
        )
    event_flag = events[...].astype(jnp.float32)

    for q in range(CHUNKS):
        def wait(i, c, q=q):
            peer = lax.rem(mf + i, n_feat)
            copy = eta_copy(q, peer, peer)
            copy.wait_recv()
            copy.wait_send()
            return c

        lax.fori_loop(1, n_feat, wait, 0)
    eta = eta_parts[0]
    for f in range(1, n_feat):
        eta = eta + eta_parts[f]
    risk = jnp.exp(eta)

    suffix = risk
    for d in SHIFTS:
        suffix = suffix + jnp.where(lane < TILE - d, pltpu.roll(suffix, TILE - d, 1), 0.0)
    pay_one[...] = jnp.sum(
        jnp.where(diagonal, suffix[:, 0:1], 0.0), axis=0, keepdims=True
    )
    sum_one[me] = pay_one[...]
    tm_send(lambda peer: pay_one, sum_one, one_send, one_recv)
    later = suffix
    for k, d in enumerate(SHIFTS):
        later = jnp.where(shifted[k] > 0.5, pltpu.roll(later, d, 1), later)
    tm_wait(lambda peer: pay_one, sum_one, one_send, one_recv)

    def add_later(c, total):
        return total + jnp.where(perm_all[c] > perm_col, sum_one[c], 0.0)

    after = lax.fori_loop(0, n_tm, add_later, jnp.zeros((rows, TILE), jnp.float32))
    risk_total = later + jnp.sum(after, axis=1, keepdims=True)
    hazard_one = event_flag / risk_total
    hazard_two = hazard_one / risk_total
    prefix_one, prefix_two = hazard_one, hazard_two
    for d in SHIFTS:
        prefix_one = prefix_one + jnp.where(lane >= d, pltpu.roll(prefix_one, d, 1), 0.0)
        prefix_two = prefix_two + jnp.where(lane >= d, pltpu.roll(prefix_two, d, 1), 0.0)
    pay_two[...] = jnp.sum(
        jnp.where(diagonal, prefix_one[:, TILE - 1 : TILE], 0.0)
        + jnp.where(lane == row + HALF, prefix_two[:, TILE - 1 : TILE], 0.0),
        axis=0, keepdims=True,
    )
    sum_two[me] = pay_two[...]
    tm_send(lambda peer: pay_two, sum_two, two_send, two_recv)
    early_one, early_two = prefix_one, prefix_two
    for k, d in enumerate(SHIFTS):
        tied = shifted[len(SHIFTS) + k] > 0.5
        early_one = jnp.where(tied, pltpu.roll(early_one, TILE - d, 1), early_one)
        early_two = jnp.where(tied, pltpu.roll(early_two, TILE - d, 1), early_two)
    tm_wait(lambda peer: pay_two, sum_two, two_send, two_recv)

    def add_early(c, total):
        return total + jnp.where(perm_all[c] < perm_col, sum_two[c], 0.0)

    before = lax.fori_loop(0, n_tm, add_early, jnp.zeros((rows, TILE), jnp.float32))
    cum_one = early_one + jnp.sum(
        jnp.where(lane < HALF, before, 0.0), axis=1, keepdims=True
    )
    cum_two = early_two + jnp.sum(
        jnp.where(lane < HALF, 0.0, before), axis=1, keepdims=True
    )
    resid_out[...] = event_flag - risk * cum_one
    weight_out[...] = risk * cum_one - risk * risk * cum_two


def gram_kernel(tiles, ids, resid, weight, total):
    step = pl.program_id(0)
    rows, slots = tiles.shape[:2]

    @pl.when(step == 0)
    def _():
        total[...] = jnp.zeros_like(total)

    for n in range(rows):
        scale = weight[n : n + 1, :]
        rounded = jnp.broadcast_to(resid[n : n + 1, :], (16, TILE)).astype(jnp.bfloat16)
        for s in range(slots):
            tile = tiles[n, s]
            turned = (tile.T.astype(jnp.float32) * scale).astype(jnp.bfloat16)
            block = ids[step * rows + n, s]
            total[block] += jnp.dot(
                jnp.concatenate([turned, rounded], axis=0), tile,
                preferred_element_type=jnp.float32,
            )


def eliminate(system, rhs):
    tiles = TILE // 8
    sub = lax.broadcasted_iota(jnp.int32, (8, TILE), 0)
    a = tuple(system[8 * i : 8 * i + 8, :] for i in range(tiles))
    g = tuple(rhs[8 * i : 8 * i + 8, :] for i in range(tiles))

    def spread(x, r):
        return jnp.broadcast_to(x[r : r + 1, :], (8, TILE))

    def panel(p, carry):
        a, g = list(carry[0]), list(carry[1])
        cols = [
            [jnp.broadcast_to(a[i][:, r : r + 1], (8, TILE)) for i in range(tiles)]
            for r in range(8)
        ]
        for r in range(8):
            inverse = 1.0 / spread(cols[r][0], r)
            factor = [c * inverse for c in cols[r]]
            factor[0] = jnp.where(sub == r, 1.0 - inverse, factor[0])
            for later in range(r + 1, 8):
                pivot = spread(cols[later][0], r)
                for i in range(tiles):
                    cols[later][i] = cols[later][i] - factor[i] * pivot
            pivot_a, pivot_g = spread(a[0], r), spread(g[0], r)
            for i in range(tiles):
                a[i] = a[i] - factor[i] * pivot_a
                g[i] = g[i] - factor[i] * pivot_g
        a = [pltpu.roll(x, TILE - 8, 1) for x in a]
        return tuple(a[1:] + a[:1]), tuple(g[1:] + g[:1])

    _, g = lax.fori_loop(0, tiles, panel, (a, g))
    return jnp.concatenate(g, axis=0)


def solve_kernel(
    n_z, n_y,
    parts, grad_out, step_out,
    packed, first, middle, second, grad_row, step_row,
    first_send, first_recv, second_send, second_recv, grad_send, grad_recv, step_send, step_recv,
):
    n_tm = n_z * n_y
    me = lax.axis_index("tm")
    mf = lax.axis_index("feat")
    z = lax.div(me, n_y)
    y = lax.rem(me, n_y)
    barrier = pltpu.get_barrier_semaphore()

    def greet(i, c):
        pl.semaphore_signal(
            barrier, inc=1, device_id=(lax.rem(me + i, n_tm), mf), device_id_type=MESH
        )
        return c

    lax.fori_loop(1, n_tm, greet, 0)
    pl.semaphore_wait(barrier, n_tm - 1)

    lane8 = lanes_of(8)
    sub8 = lax.broadcasted_iota(jnp.int32, (8, TILE), 0)

    def pack(block, to):
        whole = parts[block, 0:TILE, :]
        whole = 0.5 * (whole + whole.T)
        for i in range(7):
            width = 120 - 8 * i
            low = whole[8 * (14 - i) : 8 * (14 - i) + 8, :]
            high = pltpu.roll(whole[8 * i : 8 * i + 8, :], width, 1)
            to[8 * i : 8 * i + 8, :] = jnp.where(lane8 < width, low, high)
        grad = parts[block, TILE : TILE + 8, :]
        tail = jnp.where(sub8 == 0, grad, pltpu.roll(grad, HALF, 1))
        to[56:64, :] = jnp.where(lane8 < HALF, whole[56:64, :], tail)
        to[64:72, :] = whole[120:128, :]

    half_z = n_z // 2

    def far(k):
        return half_z + jnp.where(lax.rem(k, 2) == 1, -lax.div(k + 1, 2), lax.div(k, 2))

    def first_copy(k, dy):
        return pltpu.make_async_remote_copy(
            src_ref=packed.at[dy, k], dst_ref=first.at[dy - 1, k],
            send_sem=first_send.at[dy - 1, k], recv_sem=first_recv.at[dy - 1, k],
            device_id=(z * n_y + lax.rem(y + dy, n_y), mf), device_id_type=MESH,
        )

    def second_copy(k):
        return pltpu.make_async_remote_copy(
            src_ref=middle.at[k], dst_ref=second.at[k],
            send_sem=second_send.at[k], recv_sem=second_recv.at[k],
            device_id=(lax.rem(z + far(k), n_z) * n_y + y, mf), device_id_type=MESH,
        )

    def send_first(k, c):
        to_z = lax.rem(z + far(k), n_z)
        for dy in list(range(1, n_y)) + [0]:
            pack(to_z * n_y + lax.rem(y + dy, n_y), packed.at[dy, k])
            if dy:
                first_copy(k, dy).start()
        return c

    lax.fori_loop(0, n_z, send_first, 0)

    def gathered(k):
        for dy in range(1, n_y):
            first_copy(k, dy).wait_recv()
        total = packed[0, k]
        for dy in range(1, n_y):
            total = total + first[dy - 1, k]
        return total

    def send_second(k, c):
        middle[k] = gathered(k)
        second_copy(k).start()
        return c

    lax.fori_loop(0, n_z - 1, send_second, 0)
    total = gathered(n_z - 1)
    for k in range(n_z - 1):
        second_copy(k).wait_recv()
        total = total + second[k]

    pieces = [total[8 * i : 8 * i + 8, :] for i in range(9)]
    turned = pltpu.roll(pieces[7], HALF, 1)
    gradient = jnp.where(lane8[0:1] < HALF, turned[1:2, :], pieces[7][0:1, :])
    grad_row[...] = gradient
    grad_out[me] = gradient

    def gather_copy(i, src, dst, send_sem, recv_sem, incoming):
        peer = lax.rem(me + i, n_tm)
        at = peer if incoming else me
        return pltpu.make_async_remote_copy(
            src_ref=src, dst_ref=dst.at[at], send_sem=send_sem.at[peer], recv_sem=recv_sem.at[at],
            device_id=(peer, mf), device_id_type=MESH,
        )

    def send_grad(i, c):
        gather_copy(i, grad_row, grad_out, grad_send, grad_recv, False).start()
        return c

    lax.fori_loop(1, n_tm, send_grad, 0)

    tile_rows = [pltpu.roll(pieces[i], 8 + 8 * i, 1) for i in range(7)]
    tile_rows += [pieces[7]] + [pieces[14 - i] for i in range(8, 15)] + [pieces[8]]
    stacked = jnp.concatenate(tile_rows, axis=0)
    row = lax.broadcasted_iota(jnp.int32, (TILE, TILE), 0)
    lane = lanes_of(TILE)
    lower = jnp.where(lane <= row, stacked, 0.0)
    upper = jnp.where(lane < row, stacked, 0.0).T
    system = lower + upper + jnp.where(lane == row, 1.0, 0.0)
    column = jnp.sum(jnp.where(lane == row, gradient, 0.0), axis=1, keepdims=True)
    solved = eliminate(system, jnp.broadcast_to(column, (TILE, TILE)))
    answer = jnp.sum(jnp.where(lane == row, solved, 0.0), axis=0, keepdims=True)
    step_row[...] = answer
    step_out[me] = answer

    def send_step(i, c):
        gather_copy(i, step_row, step_out, step_send, step_recv, False).start()
        return c

    lax.fori_loop(1, n_tm, send_step, 0)
    for k in range(n_z):
        for dy in range(1, n_y):
            first_copy(k, dy).wait_send()
        if k < n_z - 1:
            second_copy(k).wait_send()

    def finish(i, c):
        for copy in (
            gather_copy(i, grad_row, grad_out, grad_send, grad_recv, True),
            gather_copy(i, step_row, step_out, step_send, step_recv, True),
        ):
            copy.wait_recv()
            copy.wait_send()
        return c

    lax.fori_loop(1, n_tm, finish, 0)


def local(tile_data, tile_ids, owner_perm, events, groups, coefficients):
    rows, slots = tile_data.shape[:2]
    n_tm, n_feat = lax.axis_size("tm"), lax.axis_size("feat")
    n_y = min(Y_SIZE, n_tm // 2)
    n_z = n_tm // n_y
    blocks = coefficients.shape[0] // TILE
    f32, vmem = jnp.float32, pl.BlockSpec(memory_space=pltpu.VMEM)
    smem, anywhere = pl.BlockSpec(memory_space=pltpu.SMEM), pl.BlockSpec(memory_space=pl.ANY)
    dma = pltpu.SemaphoreType.DMA
    coef = coefficients.astype(f32).reshape(blocks, 1, TILE)
    perm = owner_perm.astype(f32)
    perm = jnp.pad(perm, (0, HALF - rows))
    perm_row = jnp.concatenate([perm, perm]).reshape(1, TILE)

    resid, weight = pl.pallas_call(
        functools.partial(scores_kernel, n_tm, n_feat),
        out_shape=[jax.ShapeDtypeStruct((rows, TILE), f32)] * 2,
        in_specs=[anywhere, smem, vmem, vmem, vmem, vmem],
        out_specs=[vmem, vmem],
        scratch_shapes=[
            pltpu.VMEM(tile_data.shape, jnp.bfloat16),
            pltpu.VMEM((n_feat, rows, TILE), f32),
            pltpu.VMEM((n_tm, 1, TILE), f32),
            pltpu.VMEM((n_tm, 1, 2 * TILE), f32),
            pltpu.VMEM((n_tm, 1, 2 * TILE), f32),
            pltpu.VMEM((n_tm, 1, TILE), f32),
            pltpu.VMEM((n_tm, 1, TILE), f32),
            pltpu.VMEM((1, TILE), f32),
            pltpu.VMEM((1, TILE), f32),
            pltpu.VMEM((2 * len(SHIFTS), rows, TILE), f32),
            dma((CHUNKS,)),
            dma((CHUNKS, n_feat)), dma((CHUNKS, n_feat)),
            dma((n_tm,)), dma((n_tm,)), dma((n_tm,)), dma((n_tm,)),
            dma((n_tm,)), dma((n_tm,)), dma((n_tm,)), dma((n_tm,)),
        ],
        compiler_params=pltpu.CompilerParams(
            collective_id=0, has_side_effects=True, vmem_limit_bytes=40 * 2**20
        ),
        name="scores",
    )(tile_data, tile_ids, perm_row, events, groups, coef)

    group = 8
    parts = pl.pallas_call(
        gram_kernel,
        out_shape=jax.ShapeDtypeStruct((blocks, TILE + 16, TILE), f32),
        grid=(rows // group,),
        in_specs=[
            pl.BlockSpec((group, slots, TILE, TILE), lambda i: (i, 0, 0, 0)),
            smem,
            pl.BlockSpec((group, TILE), lambda i: (i, 0)),
            pl.BlockSpec((group, TILE), lambda i: (i, 0)),
        ],
        out_specs=pl.BlockSpec((blocks, TILE + 16, TILE), lambda i: (0, 0, 0)),
        compiler_params=pltpu.CompilerParams(vmem_limit_bytes=40 * 2**20),
        name="gram",
    )(tile_data, tile_ids, resid, weight)

    gradient, step = pl.pallas_call(
        functools.partial(solve_kernel, n_z, n_y),
        out_shape=[jax.ShapeDtypeStruct((n_tm, 1, TILE), f32)] * 2,
        in_specs=[vmem],
        out_specs=[vmem, vmem],
        scratch_shapes=[
            pltpu.VMEM((n_y, n_z, PACK, TILE), f32),
            pltpu.VMEM((n_y - 1, n_z, PACK, TILE), f32),
            pltpu.VMEM((n_z, PACK, TILE), f32),
            pltpu.VMEM((n_z, PACK, TILE), f32),
            pltpu.VMEM((1, TILE), f32),
            pltpu.VMEM((1, TILE), f32),
            dma((n_y - 1, n_z)), dma((n_y - 1, n_z)), dma((n_z,)), dma((n_z,)),
            dma((n_tm,)), dma((n_tm,)), dma((n_tm,)), dma((n_tm,)),
        ],
        compiler_params=pltpu.CompilerParams(
            collective_id=1, has_side_effects=True, vmem_limit_bytes=40 * 2**20
        ),
        name="solve",
    )(parts)
    return gradient.reshape(-1), step.reshape(-1)


def solution(mesh):
    return jax.shard_map(
        local,
        mesh=mesh,
        in_specs=(
            P("tm", "feat", None, None),
            P("tm", "feat"),
            P("tm"),
            P("tm", None),
            P("tm", None),
            P("feat"),
        ),
        out_specs=(P("feat"), P("feat")),
        check_vma=False,
    )
```

time: 896 us -> 96.8 us (0.11)
  blocking collectives: 455 us -> 0 us
  waiting for transfers between devices: 217 us -> 0 us
  Pallas kernels: 0 us -> 87.5 us
  other arithmetic: 66.5 us -> 1.43 us
  local copies, waits for them, and re-layouts: 52.4 us -> 6.88 us
  matrix products: 34.7 us -> 0 us
  starting transfers between devices: 31.6 us -> 0 us
  loops' own time: 21.7 us -> 0 us
  between operations: 14.3 us -> 0.66 us
    unnamed x3 -> x0, blocking collectives: 352 us -> none
    all_to_all x4 -> x0, waiting for transfers between devices: 191 us -> none  [the longest x1 177 us: local(): lax.all_to_all(outgoing[0], 'tm', split_axis=0, concat_axis=0, tiled=True)]
    pallas_call x0 -> x3, Pallas kernels: none -> 87.5 us  [the longest x1 42.4 us: local(): pl.pallas_call(functools.partial(scores_kernel, n_tm, n_feat), out_shape=...]
    all_gather x2 -> x0, blocking collectives: 78 us -> none  [the longest x1 40.1 us: local(): lax.all_gather(grad_part, 'tm', axis=0, tiled=True)]
    scatter-add x2 -> x0, other arithmetic: 34.6 us -> none  [the longest x1 33.2 us: local(): hess_local = jnp.zeros((local_blocks, tile_width, tile_width), jnp.float3...]
    dot_general x7 -> x0, matrix products: 33.7 us -> none  [the longest x1 13.4 us: local(): jnp.einsum('nspa,nspb->nsab', weighted, time_tiles, preferred_element_typ...]
    all_to_all x4 -> x0, starting transfers between devices: 31.6 us -> none  [the longest x1 11.7 us: local(): lax.all_to_all(outgoing[3], 'tm', split_axis=0, concat_axis=0, tiled=True)]
    reduce_scatter x1 -> x0, waiting for transfers between devices: 26.4 us -> none  [local(): lax.psum_scatter(hess_local, 'tm', scatter_dimension=0, tiled=True)]
  transfers between devices with their start and end apart: 5 -> 0, of which waited for: 4 -> 0; matrix products, arithmetic and copies ran while one was open for 3% -> 0% of each run, Pallas kernels for 0% -> 0%
where the time goes in v1:
time: 96.8 us; the launch traced here: 96.4 us
  Pallas kernels  87.5 us (90%)
  local copies, waits for them, and re-layouts  6.88 us (7%)
  other arithmetic  1.43 us (1%)
    pallas_call x1, Pallas kernels, local(): pl.pallas_call(functools.partial(scores_kernel, n_tm, n_feat), out_shape=...  42.4 us
    pallas_call x1, Pallas kernels, local(): pl.pallas_call(functools.partial(solve_kernel, n_z, n_y), out_shape=[jax....  37.1 us
    pallas_call x1, Pallas kernels, local(): pl.pallas_call(gram_kernel, out_shape=jax.ShapeDtypeStruct((blocks, TILE...  7.96 us
    unnamed x9, local copies, waits for them, and re-layouts  6.88 us

profile of v1, /device:TPU:8, one launch (start us, length us, event | category | flops | bytes accessed | tf_op | source)
XLA Modules:
  0.0 96.4 jit_solution(12081602905971171805)
XLA Ops:
  0.6 0.7 convert_element_type.4
  1.3 0.1 maximum_bitcast_fusion.perm_row
  1.4 0.7 reshape.23
  2.1 0.8 copy.9.ids
  2.8 0.0 copy-start
  2.8 3.4 %copy-done = bf16[64,4,128,128]{3,2,1,0:T(8,128)(2,1)S(1)} copy-done((bf16[64,4,128,128]{3,2,1,0:T(8,128)(2,1)S(1)}, bf16[64,4,128,128]{3,2,1,0:T(8,128)(2,1)}, u32[]{:S(2)}) %copy-start) | copy-done | bytes 8388632
  6.2 0.0 copy-start.1
  6.2 0.8 copy-done.1
  7.0 0.0 copy-start.2
  7.0 0.8 copy-done.2
  7.7 42.4 %scores.1 = (f32[64,128]{1,0:T(8,128)S(1)}, f32[64,128]{1,0:T(8,128)S(1)}) custom-call(bf16[64,4,128,128]{3,2,1,0:T(8,128)(2,1)S(1)} %copy-done, s32[64,4]{1,0:T(8,128)S(1)} %copy.9.ids, f32[1,128]{1,0:T(1,128)S(1)} %maximum_bitcast_fusion.perm_row, s32[64,128]{1,0:T(8,128)S(1)} %copy-done.1, s32[64,128]{1,0:T(8,128)S(1)} %copy-done.2, f32[32,1,128]{2,1,0:T(1,128)S(1)} %bitcast.5), custom_call_target="tpu_custom_call" | custom-call | tf_op jit(solution)/shard_map/scores/pallas_call | solution.py:463
  50.1 8.0 %gram.1.parts = f32[32,144,128]{2,1,0:T(8,128)S(1)} custom-call(bf16[64,4,128,128]{3,2,1,0:T(8,128)(2,1)S(1)} %copy-done, s32[64,4]{1,0:T(8,128)S(1)} %copy.9.ids, f32[64,128]{1,0:T(8,128)S(1)} %get-tuple-element.6.resid, f32[64,128]{1,0:T(8,128)S(1)} %get-tuple-element.7.weight), custom_call_target="tpu_custom_call" | custom-call | tf_op jit(solution)/shard_map/gram/pallas_call | solution.py:491
  58.1 37.1 %solve.1 = (f32[32,1,128]{2,1,0:T(1,128)S(1)}, f32[32,1,128]{2,1,0:T(1,128)S(1)}) custom-call(f32[32,144,128]{2,1,0:T(8,128)S(1)} %gram.1.parts), custom_call_target="tpu_custom_call" | custom-call | tf_op jit(solution)/shard_map/solve/pallas_call | solution.py:506
  95.2 0.6 copy.12
  95.8 0.6 copy.13
Async XLA Ops:
  2.8 3.4 %copy-start = (bf16[64,4,128,128]{3,2,1,0:T(8,128)(2,1)S(1)}, bf16[64,4,128,128]{3,2,1,0:T(8,128)(2,1)}, u32[]{:S(2)}) copy-start(bf16[64,4,128,128]{3,2,1,0:T(8,128)(2,1)} %tiles.3) | copy-start | bytes 25165828
  6.2 0.8 copy-start.1
  7.0 0.8 copy-start.2

commit v2 on v1

v2 whole, which is shorter than its diff:
```python
import functools

import jax
import jax.numpy as jnp
from jax import lax
from jax.experimental import pallas as pl
from jax.experimental.pallas import tpu as pltpu
from jax.sharding import PartitionSpec as P

MESH = pl.DeviceIdType.MESH
TILE = 128
HALF = 64
PACK = 72
SHIFTS = (1, 2, 4, 8, 16, 32, 64)
Y_SIZE = 4
CHUNKS = 4
CUT = 40
UNROLL = 18


def lanes_of(rows):
    return lax.broadcasted_iota(jnp.int32, (rows, TILE), 1)


def three_parts(x):
    high = x.astype(jnp.bfloat16)
    rest = x - high.astype(jnp.float32)
    mid = rest.astype(jnp.bfloat16)
    low = (rest - mid.astype(jnp.float32)).astype(jnp.bfloat16)
    return high, mid, low


def times_ones(x, mask):
    rows = x.shape[0]
    out = jnp.dot(
        jnp.concatenate(three_parts(x), axis=0),
        jnp.where(mask, 1.0, 0.0).astype(jnp.bfloat16),
        preferred_element_type=jnp.float32,
    )
    return out[2 * rows :] + out[rows : 2 * rows] + out[:rows]


def eliminate(system, rhs, wide=32):
    tiles = wide // 8
    sub = lax.broadcasted_iota(jnp.int32, (8, TILE), 0)

    def spread(x, r):
        return jnp.broadcast_to(x[r : r + 1, :], (8, TILE))

    def panel(p, carry):
        whole, right = carry
        a = [whole[8 * i : 8 * i + 8, :] for i in range(tiles)]
        g = [right[8 * i : 8 * i + 8, :] for i in range(tiles)]
        for q in range(tiles):
            cols = [
                [
                    jnp.broadcast_to(a[i][:, 8 * q + r : 8 * q + r + 1], (8, TILE))
                    for i in range(tiles)
                ]
                for r in range(8)
            ]
            head = [cols[r][q] for r in range(8)]
            top, top_g = a[q], g[q]
            for r in range(8):
                inverse = 1.0 / spread(head[r], r)
                factor = jnp.where(sub == r, 1.0 - inverse, head[r] * inverse)
                for k in range(r + 1, 8):
                    head[k] = head[k] - factor * spread(head[k], r)
                top = top - factor * spread(top, r)
                top_g = top_g - factor * spread(top_g, r)
            for i in range(tiles):
                if i != q:
                    for r in range(8):
                        a[i] = a[i] - cols[r][i] * spread(top, r)
                        g[i] = g[i] - cols[r][i] * spread(top_g, r)
            a[q], g[q] = top, top_g
        done, done_g = jnp.concatenate(a, axis=0), jnp.concatenate(g, axis=0)
        rest = whole[wide:, :]
        update = jnp.dot(
            rest[:, :wide], jnp.concatenate([done, done_g], axis=1),
            precision=lax.Precision.HIGHEST, preferred_element_type=jnp.float32,
        )
        whole = jnp.concatenate([rest - update[:, :TILE], done], axis=0)
        right = jnp.concatenate([right[wide:, :] - update[:, TILE:], done_g], axis=0)
        return pltpu.roll(whole, TILE - wide, 1), right

    return lax.fori_loop(0, TILE // wide, panel, (system, rhs))[1]


def newton_kernel(
    n_z, n_y, n_feat,
    tiles, ids, id_rows, perm, events, groups, coef,
    grad_out, step_out,
    held, event_buf, group_buf, perm_buf, id_buf, coef_buf, coef_wide, eta_rows,
    eta_parts, perm_all, group_send, group_recv, sum_one, sum_two,
    table_buf, table, weight_rows, resid_rows, running,
    packed, chain, ring, middle, second, grad_row, step_row,
    tile_sem, small_sem, table_sem, eta_send, eta_recv, perm_send, perm_recv, grp_send, grp_recv,
    one_send, one_recv, two_send, two_recv,
    chain_send, chain_recv, ring_send, ring_recv, second_send, second_recv,
    grad_send, grad_recv, step_send, step_recv,
):
    n_tm = n_z * n_y
    z = lax.div(lax.axis_index("tm"), n_y)
    y = lax.rem(lax.axis_index("tm"), n_y)
    me = lax.axis_index("tm")
    mf = lax.axis_index("feat")
    rows = events.shape[0]
    per = rows // CHUNKS
    slots, blocks = id_rows.shape[0], coef.shape[0]
    count = rows * slots
    barrier = pltpu.get_barrier_semaphore()

    def greet_tm(i, c):
        pl.semaphore_signal(
            barrier, inc=1, device_id=(lax.rem(me + i, n_tm), mf), device_id_type=MESH
        )
        return c

    def greet_feat(i, c):
        pl.semaphore_signal(
            barrier, inc=1, device_id=(me, lax.rem(mf + i, n_feat)), device_id_type=MESH
        )
        return c

    def tile_copy(q):
        part = pl.ds(q * per * slots, per * slots)
        return pltpu.make_async_copy(tiles.at[part], held.at[part], tile_sem.at[q])

    small = [
        pltpu.make_async_copy(source, target, small_sem.at[k])
        for k, (source, target) in enumerate(
            ((coef, coef_buf), (perm, perm_buf), (groups, group_buf), (events, event_buf), (id_rows, id_buf))
        )
    ]
    small[0].start()
    tile_copy(0).start()
    lax.fori_loop(1, n_tm, greet_tm, 0)
    lax.fori_loop(1, n_feat, greet_feat, 0)
    for q in range(1, CHUNKS):
        tile_copy(q).start()
    for copy in small[1:]:
        copy.start()

    def tm_copy(i, source, target, send_sem, recv_sem, sign):
        peer = lax.rem(me + sign * i + n_tm, n_tm)
        return pltpu.make_async_remote_copy(
            src_ref=source(i), dst_ref=target.at[i],
            send_sem=send_sem.at[i], recv_sem=recv_sem.at[i],
            device_id=(peer, mf), device_id_type=MESH,
        )

    def tm_send(*how):
        def one(i, c):
            tm_copy(i, *how).start()
            return c

        lax.fori_loop(1, n_tm, one, 0)

    def tm_wait(*how):
        def one(i, c):
            copy = tm_copy(i, *how)
            copy.wait_recv()
            copy.wait_send()
            return c

        lax.fori_loop(1, n_tm, one, 0)

    small[0].wait()
    wide = coef_buf[...].astype(jnp.float32)
    for j in range(blocks):
        coef_wide[j] = wide[j : j + 1, :]

    def eta_copy(q, i):
        part = pl.ds(q * per, per)
        return pltpu.make_async_remote_copy(
            src_ref=eta_parts.at[0, part], dst_ref=eta_parts.at[i, part],
            send_sem=eta_send.at[q, i], recv_sem=eta_recv.at[q, i],
            device_id=(me, lax.rem(mf + i, n_feat)), device_id_type=MESH,
        )

    def eta_make(q):
        tile_copy(q).wait()
        together = min(4, per)

        def some(k, c):
            for u in range(together):
                i = k * together + u
                n = q * per + i
                total = None
                for s in range(slots):
                    term = held[n * slots + s].astype(jnp.float32) * coef_wide[ids[s, n]]
                    total = term if total is None else total + term
                eta_rows[i] = jnp.sum(total.T, axis=0, keepdims=True)
            return c

        lax.fori_loop(0, per // together, some, 0)
        eta_parts[0, q * per : (q + 1) * per, :] = jnp.concatenate(
            [eta_rows[i] for i in range(per)], axis=0
        )

    def eta_start(q):
        for i in range(1, n_feat):
            eta_copy(q, i).start()

    lane = lanes_of(rows)
    row = lax.broadcasted_iota(jnp.int32, (rows, TILE), 0)
    diagonal = lane == row
    for q in range(CHUNKS - 1):
        eta_make(q)
    small[1].wait()
    gap = jnp.zeros((1, HALF - rows), jnp.int32)
    perm_all[0] = jnp.concatenate(
        [perm_buf[...], gap] * 2 if rows < HALF else [perm_buf[...]] * 2, axis=1
    )
    pl.semaphore_wait(barrier, n_tm + n_feat - 2)
    perm_how = (lambda i: perm_all.at[0], perm_all, perm_send, perm_recv, 1)
    tm_send(*perm_how)
    for q in range(CHUNKS - 1):
        eta_start(q)
    eta_make(CHUNKS - 1)
    eta_start(CHUNKS - 1)

    held[count] = jnp.zeros((TILE, TILE), jnp.bfloat16)
    resid_rows[rows] = jnp.zeros((1, TILE), jnp.float32)
    weight_rows[rows] = jnp.zeros((1, TILE), jnp.float32)
    running[running.shape[0] - 1] = jnp.zeros(running.shape[1:], jnp.float32)
    table_buf[...] = jnp.zeros_like(table_buf)

    for copy in small[2:]:
        copy.wait()
    event_flag = event_buf[...].astype(jnp.float32)
    group_bf = group_buf[...].astype(jnp.float32).astype(jnp.bfloat16)
    place = lax.broadcasted_iota(jnp.int32, (n_tm, rows), 1).astype(jnp.float32)
    perm_row = perm_all[0].astype(jnp.float32)
    perm_col = jnp.sum(jnp.where(diagonal, perm_row, 0.0), axis=1, keepdims=True)
    my_shard = jnp.floor(perm_col * (1.0 / rows))
    same = jnp.logical_and(jnp.floor(perm_row * (1.0 / rows)) == my_shard, perm_row < perm_col)
    rank = jnp.sum(
        jnp.where(jnp.logical_and(same, lane < rows), 1.0, 0.0), axis=1, keepdims=True
    )
    id_all = id_buf[...]
    block_at = lax.broadcasted_iota(jnp.int32, (blocks, rows), 0)
    row_at = lax.broadcasted_iota(jnp.int32, (blocks, rows), 1)
    present = jnp.zeros((blocks, rows), jnp.float32)
    which = jnp.zeros((blocks, rows), jnp.float32)
    for s in range(slots):
        here = id_all[s : s + 1, :] == block_at
        present = present + jnp.where(here, 1.0, 0.0)
        which = which + jnp.where(here, (row_at * slots + s).astype(jnp.float32), 0.0)
    before_row = jnp.where(
        lax.broadcasted_iota(jnp.int32, (rows, rows), 0)
        < lax.broadcasted_iota(jnp.int32, (rows, rows), 1), 1.0, 0.0,
    ).astype(jnp.bfloat16)
    rank_in = jnp.dot(present.astype(jnp.bfloat16), before_row, preferred_element_type=jnp.float32)
    rank_in = jnp.where(present > 0.5, rank_in, -1.0)
    number = jnp.sum(present, axis=1, keepdims=True)
    twos = jnp.floor((number + 1.0) * 0.5)
    square_row = lax.broadcasted_iota(jnp.int32, (blocks, blocks), 0)
    square_col = lax.broadcasted_iota(jnp.int32, (blocks, blocks), 1)
    number_row = jnp.sum(jnp.where(square_row == square_col, number, 0.0), axis=0, keepdims=True)
    twos_row = jnp.sum(jnp.where(square_row == square_col, twos, 0.0), axis=0, keepdims=True)
    start_row = jnp.sum(jnp.where(square_row < square_col, twos, 0.0), axis=0, keepdims=True)
    spot_row = lax.broadcasted_iota(jnp.int32, (TILE, TILE), 0)
    spot_col = lanes_of(TILE)
    for part in range(3):
        spot = (lax.broadcasted_iota(jnp.int32, (TILE, blocks), 0) + part * TILE).astype(jnp.float32)
        offset = spot - 2.0 * start_row
        inside = jnp.logical_and(offset >= 0.0, offset < number_row)
        member = jnp.where(inside, 1.0, 0.0).astype(jnp.bfloat16)
        wanted = jnp.sum(jnp.where(inside, offset, 0.0), axis=1, keepdims=True)
        filled = jnp.sum(jnp.where(inside, 1.0, 0.0), axis=1, keepdims=True)
        ranks = jnp.dot(member, rank_in.astype(jnp.bfloat16), preferred_element_type=jnp.float32)
        names = jnp.dot(member, which.astype(jnp.bfloat16), preferred_element_type=jnp.float32)
        chosen = jnp.sum(jnp.where(ranks == wanted, names, 0.0), axis=1, keepdims=True)
        chosen = jnp.where(filled > 0.5, jnp.minimum(chosen, 1.0 * count), 1.0 * count)
        for place_in, column in ((part, chosen), (3 + part, wanted)):
            table_buf[place_in : place_in + 1, :] = jnp.sum(
                jnp.where(spot_row == spot_col, column, 0.0), axis=0, keepdims=True
            ).astype(jnp.int32)
    empty = 1.0 * (running.shape[0] - 1)
    last_row = jnp.where(
        number_row > 0.5, jnp.minimum(start_row + twos_row - 1.0, empty), empty
    )
    table_buf[6:7, 0:blocks] = last_row.astype(jnp.int32)
    table_copy = pltpu.make_async_copy(table_buf, table, table_sem)
    table_copy.start()

    for q in range(CHUNKS):
        for i in range(1, n_feat):
            eta_copy(q, i).wait_recv()
    eta = eta_parts[lax.rem(mf, n_feat)]
    for f in range(1, n_feat):
        eta = eta + eta_parts[lax.rem(mf + n_feat - f, n_feat)]
    risk = jnp.exp(eta)
    sum_one[0] = jnp.sum(
        jnp.where(diagonal, jnp.sum(risk, axis=1, keepdims=True), 0.0), axis=0, keepdims=True
    )
    one_how = (lambda i: sum_one.at[0], sum_one, one_send, one_recv, 1)
    tm_send(*one_how)

    tm_wait(*perm_how)
    every = perm_all[:, 0, :].astype(jnp.float32)
    shard = jnp.floor(every * (1.0 / rows))
    within = every - shard * rows
    mine = jnp.logical_and(shard == me.astype(jnp.float32), lanes_of(n_tm) < rows)
    low = jnp.min(jnp.where(mine, within, 4096.0), axis=1, keepdims=True)
    high = jnp.max(jnp.where(mine, within, -1.0), axis=1, keepdims=True)
    group_low = jnp.dot(
        jnp.where(place == low, 1.0, 0.0).astype(jnp.bfloat16), group_bf,
        preferred_element_type=jnp.float32,
    )
    group_high = jnp.dot(
        jnp.where(place == high, 1.0, 0.0).astype(jnp.bfloat16), group_bf,
        preferred_element_type=jnp.float32,
    )
    for c in range(n_tm):
        group_send[c, :, 0:TILE] = group_low[c : c + 1, :]
        group_send[c, :, TILE : 2 * TILE] = group_high[c : c + 1, :]
    group_recv[0] = group_send[0]
    group_how = (lambda i: group_send.at[i], group_recv, grp_send, grp_recv, -1)
    tm_send(*group_how)

    source = lax.broadcasted_iota(jnp.int32, (TILE, TILE), 0)
    target = lanes_of(TILE)
    suffix = times_ones(risk, source >= target)
    tm_wait(*one_how)

    def add_later(c, total):
        return total + jnp.where(perm_all[c].astype(jnp.float32) > perm_col, sum_one[c], 0.0)

    after = lax.fori_loop(0, n_tm, add_later, jnp.zeros((rows, TILE), jnp.float32))
    after = jnp.sum(after, axis=1, keepdims=True)
    tm_wait(*group_how)
    shard_lane = lax.broadcasted_iota(jnp.int32, (rows, n_tm), 1).astype(jnp.float32)
    apart = my_shard - me.astype(jnp.float32)
    hit = jnp.where(shard_lane == apart + jnp.where(apart < 0.0, 1.0 * n_tm, 0.0), 1.0, 0.0)
    cohort_groups = jnp.dot(
        (hit * (1.0 - rank)).astype(jnp.bfloat16),
        group_recv[:, 0, 0:TILE].astype(jnp.bfloat16),
        preferred_element_type=jnp.float32,
    ) + jnp.dot(
        (hit * rank).astype(jnp.bfloat16),
        group_recv[:, 0, TILE : 2 * TILE].astype(jnp.bfloat16),
        preferred_element_type=jnp.float32,
    )
    later = suffix
    for k, d in enumerate(SHIFTS):
        back = pltpu.roll(cohort_groups, d, 1)
        tied = jnp.logical_and(lane >= d, back == cohort_groups)
        later = jnp.where(tied, pltpu.roll(later, d, 1), later)
    risk_total = later + after
    hazard_one = event_flag / risk_total
    hazard_two = hazard_one / risk_total
    sum_two[0] = jnp.sum(
        jnp.where(diagonal, jnp.sum(hazard_one, axis=1, keepdims=True), 0.0)
        + jnp.where(lane == row + HALF, jnp.sum(hazard_two, axis=1, keepdims=True), 0.0),
        axis=0, keepdims=True,
    )
    two_how = (lambda i: sum_two.at[0], sum_two, two_send, two_recv, 1)
    tm_send(*two_how)
    early_one = times_ones(hazard_one, source <= target)
    early_two = times_ones(hazard_two, source <= target)
    for k, d in enumerate(SHIFTS):
        ahead = pltpu.roll(cohort_groups, TILE - d, 1)
        tied = jnp.logical_and(lane < TILE - d, ahead == cohort_groups)
        early_one = jnp.where(tied, pltpu.roll(early_one, TILE - d, 1), early_one)
        early_two = jnp.where(tied, pltpu.roll(early_two, TILE - d, 1), early_two)
    tm_wait(*two_how)

    def add_early(c, total):
        return total + jnp.where(perm_all[c].astype(jnp.float32) < perm_col, sum_two[c], 0.0)

    before = lax.fori_loop(0, n_tm, add_early, jnp.zeros((rows, TILE), jnp.float32))
    cum_one = early_one + jnp.sum(
        jnp.where(lane < HALF, before, 0.0), axis=1, keepdims=True
    )
    cum_two = early_two + jnp.sum(
        jnp.where(lane < HALF, 0.0, before), axis=1, keepdims=True
    )
    resid = event_flag - risk * cum_one
    weight = risk * cum_one - risk * risk * cum_two
    for n in range(rows):
        resid_rows[n] = resid[n : n + 1, :]
        weight_rows[n] = weight[n : n + 1, :]

    table_copy.wait()
    steps = running.shape[0] - 1

    def gram_some(it, total):
        for u in range(UNROLL):
            m = it * UNROLL + u
            left, right = [], []
            for e in range(2):
                spot = 2 * m + e
                tile_at = table[lax.div(spot, TILE), lax.rem(spot, TILE)]
                tile_at = jnp.minimum(jnp.maximum(tile_at, 0), count)
                n = lax.div(tile_at, slots)
                tile = held[tile_at]
                turned = (tile.T.astype(jnp.float32) * weight_rows[n]).astype(jnp.bfloat16)
                rounded = jnp.broadcast_to(resid_rows[n], (16, TILE)).astype(jnp.bfloat16)
                left.append(jnp.concatenate([turned, rounded], axis=0))
                right.append(tile)
            keep = jnp.where(table[3 + lax.div(2 * m, TILE), lax.rem(2 * m, TILE)] > 0, 1.0, 0.0)
            total = total * keep + jnp.dot(
                jnp.concatenate(left, axis=1), jnp.concatenate(right, axis=0),
                preferred_element_type=jnp.float32,
            )
            running[m] = total
        return total

    lax.fori_loop(0, steps // UNROLL, gram_some, jnp.zeros((TILE + 16, TILE), jnp.float32))

    for q in range(CHUNKS):
        for i in range(1, n_feat):
            eta_copy(q, i).wait_send()

    lane8 = lanes_of(8)
    sub8 = lax.broadcasted_iota(jnp.int32, (8, TILE), 0)

    def pack(block, to):
        at = jnp.minimum(jnp.maximum(table[6, block], 0), steps)
        whole = running[at, 0:TILE, :]
        whole = 0.5 * (whole + whole.T)
        for i in range(7):
            width = 120 - 8 * i
            low = whole[8 * (14 - i) : 8 * (14 - i) + 8, :]
            high = pltpu.roll(whole[8 * i : 8 * i + 8, :], width, 1)
            to[8 * i : 8 * i + 8, :] = jnp.where(lane8 < width, low, high)
        grad = running[at, TILE : TILE + 8, :]
        tail = jnp.where(sub8 == 0, grad, pltpu.roll(grad, HALF, 1))
        to[56:64, :] = jnp.where(lane8 < HALF, whole[56:64, :], tail)
        to[64:72, :] = whole[120:128, :]

    half_z = n_z // 2

    def far(k):
        return half_z + jnp.where(lax.rem(k, 2) == 1, -lax.div(k + 1, 2), lax.div(k, 2))

    def pack_some(k, c):
        to_z = lax.rem(z + far(k), n_z)
        for dy in range(n_y):
            pack(to_z * n_y + lax.rem(y + dy, n_y), packed.at[k, dy])
        return c

    lax.fori_loop(0, n_z, pack_some, 0)

    half_rows = (pl.ds(0, CUT), pl.ds(CUT, PACK - CUT))
    ways = (1, n_y - 1)

    def chain_copy(k, w):
        return pltpu.make_async_remote_copy(
            src_ref=packed.at[k, 2, half_rows[w]], dst_ref=chain.at[k, half_rows[w]],
            send_sem=chain_send.at[w, k], recv_sem=chain_recv.at[w, k],
            device_id=(z * n_y + lax.rem(y + ways[w], n_y), mf), device_id_type=MESH,
        )

    def ring_copy(k, w):
        return pltpu.make_async_remote_copy(
            src_ref=packed.at[k, ways[w]], dst_ref=ring.at[w, k],
            send_sem=ring_send.at[w, k], recv_sem=ring_recv.at[w, k],
            device_id=(z * n_y + lax.rem(y + ways[w], n_y), mf), device_id_type=MESH,
        )

    def second_copy(k):
        return pltpu.make_async_remote_copy(
            src_ref=middle.at[k], dst_ref=second.at[k],
            send_sem=second_send.at[k], recv_sem=second_recv.at[k],
            device_id=(lax.rem(z + far(k), n_z) * n_y + y, mf), device_id_type=MESH,
        )

    def send_chain(k, c):
        for w in range(2):
            chain_copy(k, w).start()
        return c

    def send_ring(k, c):
        for w in range(2):
            chain_copy(k, w).wait_recv()
            packed[k, ways[w], half_rows[w], :] += chain[k, half_rows[w], :]
            ring_copy(k, w).start()
        return c

    def gathered(k):
        for w in range(2):
            ring_copy(k, w).wait_recv()
        return packed[k, 0] + ring[0, k] + ring[1, k]

    def send_second(k, c):
        middle[k] = gathered(k)
        second_copy(k).start()
        return c

    lax.fori_loop(0, n_z, send_chain, 0)
    lax.fori_loop(0, n_z, send_ring, 0)
    lax.fori_loop(0, n_z - 1, send_second, 0)
    total = gathered(n_z - 1)
    for k in range(n_z - 1):
        second_copy(k).wait_recv()
        total = total + second[k]

    pieces = [total[8 * i : 8 * i + 8, :] for i in range(9)]
    turned = pltpu.roll(pieces[7], HALF, 1)
    gradient = jnp.where(lane8[0:1] < HALF, turned[1:2, :], pieces[7][0:1, :])
    grad_row[...] = gradient
    grad_out[me] = gradient

    def gather_copy(i, src, dst, send_sem, recv_sem, incoming):
        peer = lax.rem(me + i, n_tm)
        at = peer if incoming else me
        return pltpu.make_async_remote_copy(
            src_ref=src, dst_ref=dst.at[at], send_sem=send_sem.at[peer], recv_sem=recv_sem.at[at],
            device_id=(peer, mf), device_id_type=MESH,
        )

    def send_grad(i, c):
        gather_copy(i, grad_row, grad_out, grad_send, grad_recv, False).start()
        return c

    lax.fori_loop(1, n_tm, send_grad, 0)

    tile_rows = [pltpu.roll(pieces[i], 8 + 8 * i, 1) for i in range(7)]
    tile_rows += [pieces[7]] + [pieces[14 - i] for i in range(8, 15)] + [pieces[8]]
    stacked = jnp.concatenate(tile_rows, axis=0)
    row = spot_row
    lane = spot_col
    lower = jnp.where(lane <= row, stacked, 0.0)
    upper = jnp.where(lane < row, stacked, 0.0).T
    system = lower + upper + jnp.where(lane == row, 1.0, 0.0)
    column = jnp.sum(jnp.where(lane == row, gradient, 0.0), axis=1, keepdims=True)
    solved = eliminate(system, jnp.broadcast_to(column, (TILE, TILE)))
    answer = jnp.sum(jnp.where(lane == row, solved, 0.0), axis=0, keepdims=True)
    step_row[...] = answer
    step_out[me] = answer

    def send_step(i, c):
        gather_copy(i, step_row, step_out, step_send, step_recv, False).start()
        return c

    lax.fori_loop(1, n_tm, send_step, 0)
    for k in range(n_z):
        for w in range(2):
            chain_copy(k, w).wait_send()
            ring_copy(k, w).wait_send()
        if k < n_z - 1:
            second_copy(k).wait_send()

    def finish(i, c):
        for copy in (
            gather_copy(i, grad_row, grad_out, grad_send, grad_recv, True),
            gather_copy(i, step_row, step_out, step_send, step_recv, True),
        ):
            copy.wait_recv()
            copy.wait_send()
        return c

    lax.fori_loop(1, n_tm, finish, 0)


def local(tile_data, tile_ids, owner_perm, events, groups, coefficients):
    rows, slots = tile_data.shape[:2]
    n_tm, n_feat = lax.axis_size("tm"), lax.axis_size("feat")
    n_y = Y_SIZE
    n_z = n_tm // n_y
    blocks = coefficients.shape[0] // TILE
    f32, vmem = jnp.float32, pl.BlockSpec(memory_space=pltpu.VMEM)
    smem, anywhere = pl.BlockSpec(memory_space=pltpu.SMEM), pl.BlockSpec(memory_space=pl.ANY)
    dma = pltpu.SemaphoreType.DMA
    ids = tile_ids.T
    count = rows * slots
    steps = -(-(count + blocks) // (2 * UNROLL)) * UNROLL

    gradient, step = pl.pallas_call(
        functools.partial(newton_kernel, n_z, n_y, n_feat),
        out_shape=[jax.ShapeDtypeStruct((n_tm, 1, TILE), f32)] * 2,
        in_specs=[anywhere, smem] + [anywhere] * 5,
        out_specs=[vmem, vmem],
        scratch_shapes=[
            pltpu.VMEM((count + 1, TILE, TILE), jnp.bfloat16),
            pltpu.VMEM((rows, TILE), jnp.int32),
            pltpu.VMEM((rows, TILE), jnp.int32),
            pltpu.VMEM((1, rows), jnp.int32),
            pltpu.VMEM((slots, rows), jnp.int32),
            pltpu.VMEM((blocks, TILE), jnp.bfloat16),
            pltpu.VMEM((blocks, 1, TILE), f32),
            pltpu.VMEM((rows // CHUNKS, 1, TILE), f32),
            pltpu.VMEM((n_feat, rows, TILE), f32),
            pltpu.VMEM((n_tm, 1, TILE), jnp.int32),
            pltpu.VMEM((n_tm, 1, 2 * TILE), f32),
            pltpu.VMEM((n_tm, 1, 2 * TILE), f32),
            pltpu.VMEM((n_tm, 1, TILE), f32),
            pltpu.VMEM((n_tm, 1, TILE), f32),
            pltpu.VMEM((8, TILE), jnp.int32),
            pltpu.SMEM((8, TILE), jnp.int32),
            pltpu.VMEM((rows + 1, 1, TILE), f32),
            pltpu.VMEM((rows + 1, 1, TILE), f32),
            pltpu.VMEM((steps + 1, TILE + 16, TILE), f32),
            pltpu.VMEM((n_z, n_y, PACK, TILE), f32),
            pltpu.VMEM((n_z, PACK, TILE), f32),
            pltpu.VMEM((2, n_z, PACK, TILE), f32),
            pltpu.VMEM((n_z, PACK, TILE), f32),
            pltpu.VMEM((n_z, PACK, TILE), f32),
            pltpu.VMEM((1, TILE), f32),
            pltpu.VMEM((1, TILE), f32),
            dma((CHUNKS,)), dma((5,)), dma,
            dma((CHUNKS, n_feat)), dma((CHUNKS, n_feat)),
            dma((n_tm,)), dma((n_tm,)), dma((n_tm,)), dma((n_tm,)),
            dma((n_tm,)), dma((n_tm,)), dma((n_tm,)), dma((n_tm,)),
            dma((2, n_z)), dma((2, n_z)), dma((2, n_z)), dma((2, n_z)), dma((n_z,)), dma((n_z,)),
            dma((n_tm,)), dma((n_tm,)), dma((n_tm,)), dma((n_tm,)),
        ],
        compiler_params=pltpu.CompilerParams(
            collective_id=0, has_side_effects=True, vmem_limit_bytes=60 * 2**20
        ),
        name="newton",
    )(
        tile_data.reshape(count, TILE, TILE), ids, ids, owner_perm.reshape(1, rows),
        events, groups, coefficients.reshape(blocks, TILE),
    )
    return gradient.reshape(-1), step.reshape(-1)


def solution(mesh):
    return jax.shard_map(
        local,
        mesh=mesh,
        in_specs=(
            P("tm", "feat", None, None),
            P("tm", "feat"),
            P("tm"),
            P("tm", None),
            P("tm", None),
            P("feat"),
        ),
        out_specs=(P("feat"), P("feat")),
        check_vma=False,
    )
```

time: 96.8 us -> 71.9 us (0.74)
  Pallas kernels: 87.5 us -> 68.2 us
  local copies, waits for them, and re-layouts: 6.88 us -> 2.65 us
  other arithmetic: 1.43 us -> 0 us
    pallas_call x3 -> x1, Pallas kernels: 87.5 us -> 68.2 us  [local(): pl.pallas_call(functools.partial(newton_kernel, n_z, n_y, n_feat), out_sh...]
    unnamed x9 -> x2, local copies, waits for them, and re-layouts: 6.88 us -> 2.65 us
where the time goes in v2:
time: 71.9 us; the launch traced here: 71.5 us
  Pallas kernels  68.2 us (95%)
  local copies, waits for them, and re-layouts  2.65 us (4%)
    pallas_call x1, Pallas kernels, local(): pl.pallas_call(functools.partial(newton_kernel, n_z, n_y, n_feat), out_sh...  68.2 us
    unnamed x2, local copies, waits for them, and re-layouts  2.65 us

profile of v2, /device:TPU:8, one launch (start us, length us, event | category | flops | bytes accessed | tf_op | source)
XLA Modules:
  0.0 71.5 jit_solution(5961708720204061296)
XLA Ops:
  0.6 68.2 %newton.1 = (f32[32,1,128]{2,1,0:T(1,128)}, f32[32,1,128]{2,1,0:T(1,128)}) custom-call(bf16[256,128,128]{2,1,0:T(8,128)(2,1)} %bitcast.6, s32[4,64]{1,0:T(4,128)} %bitcast.10, s32[4,64]{1,0:T(4,128)} %bitcast.11, s32[1,64]{1,0:T(1,128)} %bitcast.12, s32[64,128]{1,0:T(8,128)} %events.1, s32[64,128]{1,0:T(8,128)} %groups.1, bf16[32,128]{1,0:T(8,128)(2,1)} %bitcast.9), custom_call_target="tpu_custom_call" | custom-call | tf_op jit(solution)/shard_map/newton/pallas_call | solution.py:573
  68.9 1.3 %copy.10 = f32[4096]{0:T(1024)} copy(f32[4096]{0:T(1024)} %bitcast.8) | data formatting | bytes 32768
  70.2 1.3 %copy.11 = f32[4096]{0:T(1024)} copy(f32[4096]{0:T(1024)} %bitcast.7) | data formatting | bytes 32768

commit v3 on v2

--- a/solution.py
+++ b/solution.py
@@ -111,16 +111,17 @@
     count = rows * slots
     barrier = pltpu.get_barrier_semaphore()
 
-    def greet_tm(i, c):
-        pl.semaphore_signal(
-            barrier, inc=1, device_id=(lax.rem(me + i, n_tm), mf), device_id_type=MESH
-        )
+    def outward(k, size):
+        return size // 2 + jnp.where(lax.rem(k, 2) == 1, -lax.div(k + 1, 2), lax.div(k, 2))
+
+    def greet_tm(k, c):
+        peer = lax.rem(me + outward(k, n_tm), n_tm)
+        pl.semaphore_signal(barrier, inc=1, device_id=(peer, mf), device_id_type=MESH)
         return c
 
-    def greet_feat(i, c):
-        pl.semaphore_signal(
-            barrier, inc=1, device_id=(me, lax.rem(mf + i, n_feat)), device_id_type=MESH
-        )
+    def greet_feat(k, c):
+        peer = lax.rem(mf + outward(k, n_feat), n_feat)
+        pl.semaphore_signal(barrier, inc=1, device_id=(me, peer), device_id_type=MESH)
         return c
 
     def tile_copy(q):
@@ -133,51 +134,41 @@
             ((coef, coef_buf), (perm, perm_buf), (groups, group_buf), (events, event_buf), (id_rows, id_buf))
         )
     ]
+    lax.fori_loop(0, n_tm - 1, greet_tm, 0)
+    lax.fori_loop(0, n_feat - 1, greet_feat, 0)
     small[0].start()
-    tile_copy(0).start()
-    lax.fori_loop(1, n_tm, greet_tm, 0)
-    lax.fori_loop(1, n_feat, greet_feat, 0)
-    for q in range(1, CHUNKS):
+    for q in range(CHUNKS):
         tile_copy(q).start()
     for copy in small[1:]:
         copy.start()
 
-    def tm_copy(i, source, target, send_sem, recv_sem, sign):
-        peer = lax.rem(me + sign * i + n_tm, n_tm)
+    def tm_send(source, target, send_sem, recv_sem, sign):
+        def one(k, c):
+            i = outward(k, n_tm)
+            pltpu.make_async_remote_copy(
+                src_ref=source(i), dst_ref=target.at[i], send_sem=send_sem, recv_sem=recv_sem,
+                device_id=(lax.rem(me + sign * i + n_tm, n_tm), mf), device_id_type=MESH,
+            ).start()
+            return c
+
+        lax.fori_loop(0, n_tm - 1, one, 0)
+
+    def all_of(target, send_sem, recv_sem, size):
+        places = target.at[pl.ds(1, size - 1)]
         return pltpu.make_async_remote_copy(
-            src_ref=source(i), dst_ref=target.at[i],
-            send_sem=send_sem.at[i], recv_sem=recv_sem.at[i],
-            device_id=(peer, mf), device_id_type=MESH,
+            src_ref=places, dst_ref=places, send_sem=send_sem, recv_sem=recv_sem,
+            device_id=(lax.rem(me + 1, n_tm), mf), device_id_type=MESH,
         )
 
-    def tm_send(*how):
-        def one(i, c):
-            tm_copy(i, *how).start()
-            return c
-
-        lax.fori_loop(1, n_tm, one, 0)
-
-    def tm_wait(*how):
-        def one(i, c):
-            copy = tm_copy(i, *how)
-            copy.wait_recv()
-            copy.wait_send()
-            return c
-
-        lax.fori_loop(1, n_tm, one, 0)
+    def tm_wait(source, target, send_sem, recv_sem, sign):
+        copy = all_of(target, send_sem, recv_sem, n_tm)
+        copy.wait_recv()
+        copy.wait_send()
 
     small[0].wait()
     wide = coef_buf[...].astype(jnp.float32)
     for j in range(blocks):
         coef_wide[j] = wide[j : j + 1, :]
-
-    def eta_copy(q, i):
-        part = pl.ds(q * per, per)
-        return pltpu.make_async_remote_copy(
-            src_ref=eta_parts.at[0, part], dst_ref=eta_parts.at[i, part],
-            send_sem=eta_send.at[q, i], recv_sem=eta_recv.at[q, i],
-            device_id=(me, lax.rem(mf + i, n_feat)), device_id_type=MESH,
-        )
 
     def eta_make(q):
         tile_copy(q).wait()
@@ -199,27 +190,25 @@
             [eta_rows[i] for i in range(per)], axis=0
         )
 
-    def eta_start(q):
-        for i in range(1, n_feat):
-            eta_copy(q, i).start()
+    def eta_start(k, c):
+        i = outward(k, n_feat)
+        pltpu.make_async_remote_copy(
+            src_ref=eta_parts.at[0], dst_ref=eta_parts.at[i], send_sem=eta_send, recv_sem=eta_recv,
+            device_id=(me, lax.rem(mf + i, n_feat)), device_id_type=MESH,
+        ).start()
+        return c
 
     lane = lanes_of(rows)
     row = lax.broadcasted_iota(jnp.int32, (rows, TILE), 0)
     diagonal = lane == row
-    for q in range(CHUNKS - 1):
+    for q in range(CHUNKS):
         eta_make(q)
-    small[1].wait()
+    for copy in small[1:]:
+        copy.wait()
     gap = jnp.zeros((1, HALF - rows), jnp.int32)
     perm_all[0] = jnp.concatenate(
         [perm_buf[...], gap] * 2 if rows < HALF else [perm_buf[...]] * 2, axis=1
     )
-    pl.semaphore_wait(barrier, n_tm + n_feat - 2)
-    perm_how = (lambda i: perm_all.at[0], perm_all, perm_send, perm_recv, 1)
-    tm_send(*perm_how)
-    for q in range(CHUNKS - 1):
-        eta_start(q)
-    eta_make(CHUNKS - 1)
-    eta_start(CHUNKS - 1)
 
     held[count] = jnp.zeros((TILE, TILE), jnp.bfloat16)
     resid_rows[rows] = jnp.zeros((1, TILE), jnp.float32)
@@ -227,8 +216,6 @@
     running[running.shape[0] - 1] = jnp.zeros(running.shape[1:], jnp.float32)
     table_buf[...] = jnp.zeros_like(table_buf)
 
-    for copy in small[2:]:
-        copy.wait()
     event_flag = event_buf[...].astype(jnp.float32)
     group_bf = group_buf[...].astype(jnp.float32).astype(jnp.bfloat16)
     place = lax.broadcasted_iota(jnp.int32, (n_tm, rows), 1).astype(jnp.float32)
@@ -286,9 +273,15 @@
     table_copy = pltpu.make_async_copy(table_buf, table, table_sem)
     table_copy.start()
 
-    for q in range(CHUNKS):
-        for i in range(1, n_feat):
-            eta_copy(q, i).wait_recv()
+    pl.semaphore_wait(barrier, n_tm + n_feat - 2)
+    lax.fori_loop(0, n_feat - 1, eta_start, 0)
+    perm_how = (lambda i: perm_all.at[0], perm_all, perm_send, perm_recv, 1)
+    tm_send(*perm_how)
+
+    if n_feat > 1:
+        eta_all = all_of(eta_parts, eta_send, eta_recv, n_feat)
+        eta_all.wait_recv()
+        eta_all.wait_send()
     eta = eta_parts[lax.rem(mf, n_feat)]
     for f in range(1, n_feat):
         eta = eta + eta_parts[lax.rem(mf + n_feat - f, n_feat)]
@@ -411,10 +404,6 @@
 
     lax.fori_loop(0, steps // UNROLL, gram_some, jnp.zeros((TILE + 16, TILE), jnp.float32))
 
-    for q in range(CHUNKS):
-        for i in range(1, n_feat):
-            eta_copy(q, i).wait_send()
-
     lane8 = lanes_of(8)
     sub8 = lax.broadcasted_iota(jnp.int32, (8, TILE), 0)
 
@@ -437,13 +426,8 @@
     def far(k):
         return half_z + jnp.where(lax.rem(k, 2) == 1, -lax.div(k + 1, 2), lax.div(k, 2))
 
-    def pack_some(k, c):
-        to_z = lax.rem(z + far(k), n_z)
-        for dy in range(n_y):
-            pack(to_z * n_y + lax.rem(y + dy, n_y), packed.at[k, dy])
-        return c
-
-    lax.fori_loop(0, n_z, pack_some, 0)
+    def pack_for(k, dy):
+        pack(lax.rem(z + far(k), n_z) * n_y + lax.rem(y + dy, n_y), packed.at[k, dy])
 
     half_rows = (pl.ds(0, CUT), pl.ds(CUT, PACK - CUT))
     ways = (1, n_y - 1)
@@ -451,36 +435,43 @@
     def chain_copy(k, w):
         return pltpu.make_async_remote_copy(
             src_ref=packed.at[k, 2, half_rows[w]], dst_ref=chain.at[k, half_rows[w]],
-            send_sem=chain_send.at[w, k], recv_sem=chain_recv.at[w, k],
+            send_sem=chain_send.at[w], recv_sem=chain_recv.at[w, k],
             device_id=(z * n_y + lax.rem(y + ways[w], n_y), mf), device_id_type=MESH,
         )
 
     def ring_copy(k, w):
         return pltpu.make_async_remote_copy(
             src_ref=packed.at[k, ways[w]], dst_ref=ring.at[w, k],
-            send_sem=ring_send.at[w, k], recv_sem=ring_recv.at[w, k],
+            send_sem=ring_send.at[w], recv_sem=ring_recv.at[w, k],
             device_id=(z * n_y + lax.rem(y + ways[w], n_y), mf), device_id_type=MESH,
         )
 
     def second_copy(k):
         return pltpu.make_async_remote_copy(
             src_ref=middle.at[k], dst_ref=second.at[k],
-            send_sem=second_send.at[k], recv_sem=second_recv.at[k],
+            send_sem=second_send, recv_sem=second_recv,
             device_id=(lax.rem(z + far(k), n_z) * n_y + y, mf), device_id_type=MESH,
         )
 
     def send_chain(k, c):
+        pack_for(k, 2)
         for w in range(2):
             chain_copy(k, w).start()
         return c
 
     def send_ring(k, c):
+        pack_for(k, 1)
+        pack_for(k, 3)
         for w in range(2):
             chain_copy(k, w).wait_recv()
             packed[k, ways[w], half_rows[w], :] += chain[k, half_rows[w], :]
             ring_copy(k, w).start()
         return c
 
+    def pack_own(k, c):
+        pack_for(k, 0)
+        return c
+
     def gathered(k):
         for w in range(2):
             ring_copy(k, w).wait_recv()
@@ -493,10 +484,12 @@
 
     lax.fori_loop(0, n_z, send_chain, 0)
     lax.fori_loop(0, n_z, send_ring, 0)
+    lax.fori_loop(0, n_z, pack_own, 0)
     lax.fori_loop(0, n_z - 1, send_second, 0)
     total = gathered(n_z - 1)
+    second_all = all_of(second, second_send, second_recv, n_z)
+    second_all.wait_recv()
     for k in range(n_z - 1):
-        second_copy(k).wait_recv()
         total = total + second[k]
 
     pieces = [total[8 * i : 8 * i + 8, :] for i in range(9)]
@@ -505,19 +498,18 @@
     grad_row[...] = gradient
     grad_out[me] = gradient
 
-    def gather_copy(i, src, dst, send_sem, recv_sem, incoming):
-        peer = lax.rem(me + i, n_tm)
-        at = peer if incoming else me
-        return pltpu.make_async_remote_copy(
-            src_ref=src, dst_ref=dst.at[at], send_sem=send_sem.at[peer], recv_sem=recv_sem.at[at],
-            device_id=(peer, mf), device_id_type=MESH,
-        )
-
-    def send_grad(i, c):
-        gather_copy(i, grad_row, grad_out, grad_send, grad_recv, False).start()
-        return c
-
-    lax.fori_loop(1, n_tm, send_grad, 0)
+    def send_block(source, target, send_sem, recv_sem):
+        def one(k, c):
+            peer = lax.rem(me + outward(k, n_tm), n_tm)
+            pltpu.make_async_remote_copy(
+                src_ref=source, dst_ref=target.at[me], send_sem=send_sem, recv_sem=recv_sem,
+                device_id=(peer, mf), device_id_type=MESH,
+            ).start()
+            return c
+
+        lax.fori_loop(0, n_tm - 1, one, 0)
+
+    send_block(grad_row, grad_out, grad_send, grad_recv)
 
     tile_rows = [pltpu.roll(pieces[i], 8 + 8 * i, 1) for i in range(7)]
     tile_rows += [pieces[7]] + [pieces[14 - i] for i in range(8, 15)] + [pieces[8]]
@@ -533,28 +525,23 @@
     step_row[...] = answer
     step_out[me] = answer
 
-    def send_step(i, c):
-        gather_copy(i, step_row, step_out, step_send, step_recv, False).start()
-        return c
-
-    lax.fori_loop(1, n_tm, send_step, 0)
-    for k in range(n_z):
-        for w in range(2):
-            chain_copy(k, w).wait_send()
-            ring_copy(k, w).wait_send()
-        if k < n_z - 1:
-            second_copy(k).wait_send()
-
-    def finish(i, c):
-        for copy in (
-            gather_copy(i, grad_row, grad_out, grad_send, grad_recv, True),
-            gather_copy(i, step_row, step_out, step_send, step_recv, True),
+    send_block(step_row, step_out, step_send, step_recv)
+    for w in range(2):
+        for sent, send_sem, recv_sem in (
+            (chain.at[pl.ds(0, n_z), half_rows[w]], chain_send.at[w], chain_recv.at[w, 0]),
+            (ring.at[w], ring_send.at[w], ring_recv.at[w, 0]),
         ):
-            copy.wait_recv()
-            copy.wait_send()
-        return c
-
-    lax.fori_loop(1, n_tm, finish, 0)
+            pltpu.make_async_remote_copy(
+                src_ref=sent, dst_ref=sent, send_sem=send_sem, recv_sem=recv_sem,
+                device_id=(lax.rem(me + 1, n_tm), mf), device_id_type=MESH,
+            ).wait_send()
+    second_all.wait_send()
+    for target, send_sem, recv_sem in (
+        (grad_out, grad_send, grad_recv), (step_out, step_send, step_recv),
+    ):
+        copy = all_of(target, send_sem, recv_sem, n_tm)
+        copy.wait_recv()
+        copy.wait_send()
 
 
 def local(tile_data, tile_ids, owner_perm, events, groups, coefficients):
@@ -603,11 +590,9 @@
             pltpu.VMEM((1, TILE), f32),
             pltpu.VMEM((1, TILE), f32),
             dma((CHUNKS,)), dma((5,)), dma,
-            dma((CHUNKS, n_feat)), dma((CHUNKS, n_feat)),
-            dma((n_tm,)), dma((n_tm,)), dma((n_tm,)), dma((n_tm,)),
-            dma((n_tm,)), dma((n_tm,)), dma((n_tm,)), dma((n_tm,)),
-            dma((2, n_z)), dma((2, n_z)), dma((2, n_z)), dma((2, n_z)), dma((n_z,)), dma((n_z,)),
-            dma((n_tm,)), dma((n_tm,)), dma((n_tm,)), dma((n_tm,)),
+            dma, dma, dma, dma, dma, dma, dma, dma, dma, dma,
+            dma((2,)), dma((2, n_z)), dma((2,)), dma((2, n_z)), dma, dma,
+            dma, dma, dma, dma,
         ],
         compiler_params=pltpu.CompilerParams(
             collective_id=0, has_side_effects=True, vmem_limit_bytes=60 * 2**20

time: 71.9 us -> 66.1 us (0.919)
  Pallas kernels: 68.2 us -> 62.4 us
    pallas_call x1, Pallas kernels: 68.2 us -> 62.4 us  [local(): pl.pallas_call(functools.partial(newton_kernel, n_z, n_y, n_feat), out_sh...]
where the time goes in v3:
time: 66.1 us; the launch traced here: 65.7 us
  Pallas kernels  62.4 us (94%)
  local copies, waits for them, and re-layouts  2.65 us (4%)
    pallas_call x1, Pallas kernels, local(): pl.pallas_call(functools.partial(newton_kernel, n_z, n_y, n_feat), out_sh...  62.4 us
    unnamed x2, local copies, waits for them, and re-layouts  2.65 us

profile of v3, /device:TPU:8, one launch (start us, length us, event | category | flops | bytes accessed | tf_op | source)
XLA Modules:
  0.0 65.7 jit_solution(18307395393403158119)
XLA Ops:
  0.6 62.4 %newton.1 = (f32[32,1,128]{2,1,0:T(1,128)}, f32[32,1,128]{2,1,0:T(1,128)}) custom-call(bf16[256,128,128]{2,1,0:T(8,128)(2,1)} %bitcast.6, s32[4,64]{1,0:T(4,128)} %bitcast.10, s32[4,64]{1,0:T(4,128)} %bitcast.11, s32[1,64]{1,0:T(1,128)} %bitcast.12, s32[64,128]{1,0:T(8,128)} %events.1, s32[64,128]{1,0:T(8,128)} %groups.1, bf16[32,128]{1,0:T(8,128)(2,1)} %bitcast.9), custom_call_target="tpu_custom_call" | custom-call | tf_op jit(solution)/shard_map/newton/pallas_call | solution.py:560
  63.1 1.3 %copy.10 = f32[4096]{0:T(1024)} copy(f32[4096]{0:T(1024)} %bitcast.8) | data formatting | bytes 32768
  64.4 1.3 %copy.11 = f32[4096]{0:T(1024)} copy(f32[4096]{0:T(1024)} %bitcast.7) | data formatting | bytes 32768

commit v4 on v3

--- a/solution.py
+++ b/solution.py
@@ -63,11 +63,14 @@
             top, top_g = a[q], g[q]
             for r in range(8):
                 inverse = 1.0 / spread(head[r], r)
-                factor = jnp.where(sub == r, 1.0 - inverse, head[r] * inverse)
+                factor = jnp.where(sub == r, inverse, -(head[r] * inverse))
+
+                def step(x, r=r, factor=factor):
+                    return jnp.where(sub == r, 0.0, x) + factor * spread(x, r)
+
                 for k in range(r + 1, 8):
-                    head[k] = head[k] - factor * spread(head[k], r)
-                top = top - factor * spread(top, r)
-                top_g = top_g - factor * spread(top_g, r)
+                    head[k] = step(head[k])
+                top, top_g = step(top), step(top_g)
             for i in range(tiles):
                 if i != q:
                     for r in range(8):
@@ -92,13 +95,13 @@
     tiles, ids, id_rows, perm, events, groups, coef,
     grad_out, step_out,
     held, event_buf, group_buf, perm_buf, id_buf, coef_buf, coef_wide, eta_rows,
-    eta_parts, perm_all, group_send, group_recv, sum_one, sum_two,
+    eta_parts, eta_chips, perm_all, group_send, group_recv, sum_one, sum_two,
     table_buf, table, weight_rows, resid_rows, running,
     packed, chain, ring, middle, second, grad_row, step_row,
-    tile_sem, small_sem, table_sem, eta_send, eta_recv, perm_send, perm_recv, grp_send, grp_recv,
+    tile_sem, small_sem, table_sem, pair_send, pair_recv, eta_send, eta_recv, perm_send, perm_recv, grp_send, grp_recv,
     one_send, one_recv, two_send, two_recv,
     chain_send, chain_recv, ring_send, ring_recv, second_send, second_recv,
-    grad_send, grad_recv, step_send, step_recv,
+    grad_send, grad_recv, step_send, step_recv, own_sem,
 ):
     n_tm = n_z * n_y
     z = lax.div(lax.axis_index("tm"), n_y)
@@ -190,13 +193,23 @@
             [eta_rows[i] for i in range(per)], axis=0
         )
 
-    def eta_start(k, c):
-        i = outward(k, n_feat)
+    chips = n_feat // 2
+    chip, core = lax.div(mf, 2), lax.rem(mf, 2)
+    my_half = pl.ds(pl.multiple_of(core * (rows // 2), 8), rows // 2)
+
+    def pair_copy():
+        return pltpu.make_async_remote_copy(
+            src_ref=eta_parts.at[0], dst_ref=eta_parts.at[1],
+            send_sem=pair_send, recv_sem=pair_recv,
+            device_id=(me, chip * 2 + 1 - core), device_id_type=MESH,
+        )
+
+    def chip_send(d, to_core):
         pltpu.make_async_remote_copy(
-            src_ref=eta_parts.at[0], dst_ref=eta_parts.at[i], send_sem=eta_send, recv_sem=eta_recv,
-            device_id=(me, lax.rem(mf + i, n_feat)), device_id_type=MESH,
+            src_ref=eta_chips.at[0, my_half], dst_ref=eta_chips.at[d, my_half],
+            send_sem=eta_send, recv_sem=eta_recv,
+            device_id=(me, lax.rem(chip + d, chips) * 2 + to_core), device_id_type=MESH,
         ).start()
-        return c
 
     lane = lanes_of(rows)
     row = lax.broadcasted_iota(jnp.int32, (rows, TILE), 0)
@@ -274,17 +287,23 @@
     table_copy.start()
 
     pl.semaphore_wait(barrier, n_tm + n_feat - 2)
-    lax.fori_loop(0, n_feat - 1, eta_start, 0)
+    pair_copy().start()
     perm_how = (lambda i: perm_all.at[0], perm_all, perm_send, perm_recv, 1)
     tm_send(*perm_how)
 
-    if n_feat > 1:
-        eta_all = all_of(eta_parts, eta_send, eta_recv, n_feat)
+    pair_copy().wait_recv()
+    eta_chips[0] = eta_parts[0] + eta_parts[1]
+    for d in sorted(range(1, chips), key=lambda d: -min(d, chips - d)):
+        chip_send(d, 0)
+        chip_send(d, 1)
+    pair_copy().wait_send()
+    if chips > 1:
+        eta_all = all_of(eta_chips, eta_send, eta_recv, chips)
         eta_all.wait_recv()
         eta_all.wait_send()
-    eta = eta_parts[lax.rem(mf, n_feat)]
-    for f in range(1, n_feat):
-        eta = eta + eta_parts[lax.rem(mf + n_feat - f, n_feat)]
+    eta = eta_chips[lax.rem(chip, chips)]
+    for c in range(1, chips):
+        eta = eta + eta_chips[lax.rem(chip + chips - c, chips)]
     risk = jnp.exp(eta)
     sum_one[0] = jnp.sum(
         jnp.where(diagonal, jnp.sum(risk, axis=1, keepdims=True), 0.0), axis=0, keepdims=True
@@ -496,7 +515,8 @@
     turned = pltpu.roll(pieces[7], HALF, 1)
     gradient = jnp.where(lane8[0:1] < HALF, turned[1:2, :], pieces[7][0:1, :])
     grad_row[...] = gradient
-    grad_out[me] = gradient
+    own_grad = pltpu.make_async_copy(grad_row, grad_out.at[me], own_sem.at[0])
+    own_grad.start()
 
     def send_block(source, target, send_sem, recv_sem):
         def one(k, c):
@@ -523,7 +543,8 @@
     solved = eliminate(system, jnp.broadcast_to(column, (TILE, TILE)))
     answer = jnp.sum(jnp.where(lane == row, solved, 0.0), axis=0, keepdims=True)
     step_row[...] = answer
-    step_out[me] = answer
+    own_step = pltpu.make_async_copy(step_row, step_out.at[me], own_sem.at[1])
+    own_step.start()
 
     send_block(step_row, step_out, step_send, step_recv)
     for w in range(2):
@@ -536,12 +557,25 @@
                 device_id=(lax.rem(me + 1, n_tm), mf), device_id_type=MESH,
             ).wait_send()
     second_all.wait_send()
+    own_grad.wait()
+    own_step.wait()
     for target, send_sem, recv_sem in (
         (grad_out, grad_send, grad_recv), (step_out, step_send, step_recv),
     ):
         copy = all_of(target, send_sem, recv_sem, n_tm)
         copy.wait_recv()
         copy.wait_send()
+
+
+def hand_over_kernel(grad_in, step_in, grad_out, step_out, sems):
+    copies = [
+        pltpu.make_async_copy(source, target, sems.at[k])
+        for k, (source, target) in enumerate(((grad_in, grad_out), (step_in, step_out)))
+    ]
+    for copy in copies:
+        copy.start()
+    for copy in copies:
+        copy.wait()
 
 
 def local(tile_data, tile_ids, owner_perm, events, groups, coefficients):
@@ -561,7 +595,7 @@
         functools.partial(newton_kernel, n_z, n_y, n_feat),
         out_shape=[jax.ShapeDtypeStruct((n_tm, 1, TILE), f32)] * 2,
         in_specs=[anywhere, smem] + [anywhere] * 5,
-        out_specs=[vmem, vmem],
+        out_specs=[anywhere, anywhere],
         scratch_shapes=[
             pltpu.VMEM((count + 1, TILE, TILE), jnp.bfloat16),
             pltpu.VMEM((rows, TILE), jnp.int32),
@@ -571,7 +605,8 @@
             pltpu.VMEM((blocks, TILE), jnp.bfloat16),
             pltpu.VMEM((blocks, 1, TILE), f32),
             pltpu.VMEM((rows // CHUNKS, 1, TILE), f32),
-            pltpu.VMEM((n_feat, rows, TILE), f32),
+            pltpu.VMEM((2, rows, TILE), f32),
+            pltpu.VMEM((n_feat // 2, rows, TILE), f32),
             pltpu.VMEM((n_tm, 1, TILE), jnp.int32),
             pltpu.VMEM((n_tm, 1, 2 * TILE), f32),
             pltpu.VMEM((n_tm, 1, 2 * TILE), f32),
@@ -590,9 +625,9 @@
             pltpu.VMEM((1, TILE), f32),
             pltpu.VMEM((1, TILE), f32),
             dma((CHUNKS,)), dma((5,)), dma,
-            dma, dma, dma, dma, dma, dma, dma, dma, dma, dma,
+            dma, dma, dma, dma, dma, dma, dma, dma, dma, dma, dma, dma,
             dma((2,)), dma((2, n_z)), dma((2,)), dma((2, n_z)), dma, dma,
-            dma, dma, dma, dma,
+            dma, dma, dma, dma, dma((2,)),
         ],
         compiler_params=pltpu.CompilerParams(
             collective_id=0, has_side_effects=True, vmem_limit_bytes=60 * 2**20
@@ -602,6 +637,15 @@
         tile_data.reshape(count, TILE, TILE), ids, ids, owner_perm.reshape(1, rows),
         events, groups, coefficients.reshape(blocks, TILE),
     )
+    gradient, step = pl.pallas_call(
+        hand_over_kernel,
+        out_shape=[jax.ShapeDtypeStruct((n_tm, TILE), f32)] * 2,
+        in_specs=[anywhere] * 2,
+        out_specs=[anywhere] * 2,
+        scratch_shapes=[dma((2,))],
+        compiler_params=pltpu.CompilerParams(vmem_limit_bytes=60 * 2**20),
+        name="hand_over",
+    )(gradient.reshape(n_tm, TILE), step.reshape(n_tm, TILE))
     return gradient.reshape(-1), step.reshape(-1)
 
 

time: 66.1 us -> 64.5 us (0.976)
  local copies, waits for them, and re-layouts: 2.65 us -> 0 us
  Pallas kernels: 62.4 us -> 63.7 us
    unnamed x2 -> x0, local copies, waits for them, and re-layouts: 2.65 us -> none
    pallas_call x0 -> x1, Pallas kernels: none -> 2.11 us  [local(): pl.pallas_call(hand_over_kernel, out_shape=[jax.ShapeDtypeStruct((n_tm, T...]
    pallas_call x1, Pallas kernels: 62.4 us -> 61.5 us  [local(): pl.pallas_call(functools.partial(newton_kernel, n_z, n_y, n_feat), out_sh...]
where the time goes in v4:
time: 64.5 us; the launch traced here: 64.3 us
  Pallas kernels  63.7 us (99%)
    pallas_call x1, Pallas kernels, local(): pl.pallas_call(functools.partial(newton_kernel, n_z, n_y, n_feat), out_sh...  61.5 us
    pallas_call x1, Pallas kernels, local(): pl.pallas_call(hand_over_kernel, out_shape=[jax.ShapeDtypeStruct((n_tm, T...  2.11 us

profile of v4, /device:TPU:8, one launch (start us, length us, event | category | flops | bytes accessed | tf_op | source)
XLA Modules:
  0.0 64.3 jit_solution(10818986288138550202)
XLA Ops:
  0.6 61.5 %newton.1 = (f32[32,1,128]{2,1,0:T(1,128)}, f32[32,1,128]{2,1,0:T(1,128)}) custom-call(bf16[256,128,128]{2,1,0:T(8,128)(2,1)} %bitcast.8, s32[4,64]{1,0:T(4,128)} %bitcast.12, s32[4,64]{1,0:T(4,128)} %bitcast.13, s32[1,64]{1,0:T(1,128)} %bitcast.14, s32[64,128]{1,0:T(8,128)} %events.1, s32[64,128]{1,0:T(8,128)} %groups.1, bf16[32,128]{1,0:T(8,128)(2,1)} %bitcast.11), custom_call_target="tpu_custom_call" | custom-call | tf_op jit(solution)/shard_map/newton/pallas_call | solution.py:594
  62.2 2.1 %hand_over.1 = (f32[32,128]{1,0:T(8,128)}, f32[32,128]{1,0:T(8,128)}) custom-call(f32[32,128]{1,0:T(8,128)} %bitcast.9, f32[32,128]{1,0:T(8,128)} %bitcast.10), custom_call_target="tpu_custom_call" | custom-call | tf_op jit(solution)/shard_map/hand_over/pallas_call | solution.py:640

commit v5 on v4

--- a/solution.py
+++ b/solution.py
@@ -15,7 +15,7 @@
 Y_SIZE = 4
 CHUNKS = 4
 CUT = 40
-UNROLL = 18
+UNROLL = 36
 
 
 def lanes_of(rows):
@@ -341,7 +341,9 @@
     def add_later(c, total):
         return total + jnp.where(perm_all[c].astype(jnp.float32) > perm_col, sum_one[c], 0.0)
 
-    after = lax.fori_loop(0, n_tm, add_later, jnp.zeros((rows, TILE), jnp.float32))
+    after = lax.fori_loop(
+        0, n_tm, add_later, jnp.zeros((rows, TILE), jnp.float32), unroll=8
+    )
     after = jnp.sum(after, axis=1, keepdims=True)
     tm_wait(*group_how)
     shard_lane = lax.broadcasted_iota(jnp.int32, (rows, n_tm), 1).astype(jnp.float32)
@@ -383,7 +385,9 @@
     def add_early(c, total):
         return total + jnp.where(perm_all[c].astype(jnp.float32) < perm_col, sum_two[c], 0.0)
 
-    before = lax.fori_loop(0, n_tm, add_early, jnp.zeros((rows, TILE), jnp.float32))
+    before = lax.fori_loop(
+        0, n_tm, add_early, jnp.zeros((rows, TILE), jnp.float32), unroll=8
+    )
     cum_one = early_one + jnp.sum(
         jnp.where(lane < HALF, before, 0.0), axis=1, keepdims=True
     )

time: 64.5 us -> 63.6 us (0.986)
  Pallas kernels: 63.7 us -> 62.7 us
    pallas_call x1, Pallas kernels: 61.5 us -> 60.6 us  [local(): pl.pallas_call(functools.partial(newton_kernel, n_z, n_y, n_feat), out_sh...]
where the time goes in v5:
time: 63.6 us; the launch traced here: 63.4 us
  Pallas kernels  62.7 us (99%)
  between operations  0.64 us (1%)
    pallas_call x1, Pallas kernels, local(): pl.pallas_call(functools.partial(newton_kernel, n_z, n_y, n_feat), out_sh...  60.6 us
    pallas_call x1, Pallas kernels, local(): pl.pallas_call(hand_over_kernel, out_shape=[jax.ShapeDtypeStruct((n_tm, T...  2.11 us

profile of v5, /device:TPU:8, one launch (start us, length us, event | category | flops | bytes accessed | tf_op | source)
XLA Modules:
  0.0 63.4 jit_solution(7383303135369971325)
XLA Ops:
  0.6 60.6 %newton.1 = (f32[32,1,128]{2,1,0:T(1,128)}, f32[32,1,128]{2,1,0:T(1,128)}) custom-call(bf16[256,128,128]{2,1,0:T(8,128)(2,1)} %bitcast.8, s32[4,64]{1,0:T(4,128)} %bitcast.12, s32[4,64]{1,0:T(4,128)} %bitcast.13, s32[1,64]{1,0:T(1,128)} %bitcast.14, s32[64,128]{1,0:T(8,128)} %events.1, s32[64,128]{1,0:T(8,128)} %groups.1, bf16[32,128]{1,0:T(8,128)(2,1)} %bitcast.11), custom_call_target="tpu_custom_call" | custom-call | tf_op jit(solution)/shard_map/newton/pallas_call | solution.py:598
  61.3 2.1 %hand_over.1 = (f32[32,128]{1,0:T(8,128)}, f32[32,128]{1,0:T(8,128)}) custom-call(f32[32,128]{1,0:T(8,128)} %bitcast.9, f32[32,128]{1,0:T(8,128)} %bitcast.10), custom_call_target="tpu_custom_call" | custom-call | tf_op jit(solution)/shard_map/hand_over/pallas_call | solution.py:644
